TPU v7x, 32 devices: a whole 2x2x4 slice. The times are simulated.
32 devices in a mesh: dp: 4 (over z), blk: 8 (over y, x, core).
Axes of the slice: x: 2, y: 2, z: 4, core: 2. Of those that a mesh axis runs over, the one named last changes fastest.
Arguments:
- inputs: bfloat16 [4, 1024, 768], P('dp', 'blk'), may hold values from -6 to 6
- crops: int32 [4, 1024], P('dp'), may hold values from 0 to 3, as said below
- ln1_gain: float32 [768], replicated, may hold values from 0.1 to 1.9
- ln1_bias: float32 [768], replicated, may hold values from -3 to 3
- w_qkv: bfloat16 [768, 2304], replicated, may hold values from -0.21875 to 0.21875
- w_proj: bfloat16 [768, 768], replicated, may hold values from -1.75 to 1.75
- ln2_gain: float32 [768], replicated, may hold values from 0.1 to 1.9
- ln2_bias: float32 [768], replicated, may hold values from -3 to 3
- w_fc1: bfloat16 [768, 3072], replicated, may hold values from -0.21875 to 0.21875
- w_fc2: bfloat16 [3072, 768], replicated, may hold values from -0.109375 to 0.109375
- cotangent: bfloat16 [4, 1024, 768], P('dp', 'blk'), may hold values from -6 to 6
Outputs:
- output: bfloat16 [4, 1024, 768], P('dp', 'blk')
- grad_input: bfloat16 [4, 1024, 768], P('dp', 'blk')
- grad_qkv: float32 [768, 2304], P('blk')
- grad_proj: float32 [768, 768], P('blk')
- grad_fc1: float32 [768, 3072], P('blk')
- grad_fc2: float32 [3072, 768], P('blk')
- grad_ln1_gain: float32 [768], P('blk')
- grad_ln1_bias: float32 [768], P('blk')
- grad_ln2_gain: float32 [768], P('blk')
- grad_ln2_bias: float32 [768], P('blk')
Inputs may be any that keep to these rules, and one draw needn't show every extreme that they name: `crops`: crop numbers are constant on aligned runs of 128 positions, and each crop of a sequence holds 256 positions.
All inputs are finite; a program needn't handle non-finite values.
Results may differ from a plain program's by a relative error of at most 0.019.
Values may be sent and summed in bfloat16 or wider, within the bound.
A program may use at most 192 MiB of HBM per device.

v0:
```python
import math

import jax
import jax.numpy as jnp
from jax import lax
from jax.sharding import PartitionSpec as P

HEADS = 12


EPSILON = 1e-05
MASKED = -1e30


def layer_norm(values_in, gain_in, shift_in):
    row_mean = jnp.mean(values_in, axis=-1, keepdims=True)
    centred = values_in - row_mean
    row_var = jnp.mean(centred * centred, axis=-1, keepdims=True)
    return centred * lax.rsqrt(row_var + EPSILON) * gain_in + shift_in


def contract_rows(left_side, right_side):
    return lax.dot_general(
        left_side, right_side, (((0,), (0,)), ((), ())), preferred_element_type=jnp.float32
    )


def against_weight(grad_rows, weight_mat):
    return lax.dot_general(
        grad_rows, weight_mat, (((1,), (1,)), ((), ())), preferred_element_type=jnp.float32
    )


def head_view(matrix, head_count):
    return matrix.reshape(matrix.shape[0], head_count, matrix.shape[1] // head_count)


def scores_of(query_heads, key_heads, score_scale):
    return (
        jnp.einsum("qhd,khd->hqk", query_heads, key_heads, preferred_element_type=jnp.float32)
        * score_scale
    )


def weights_of(scores, visible, logsum):
    return jnp.where(visible[None], jnp.exp(scores - logsum[:, :, None]), 0.0)


def shards(
    inputs, crops, ln1_gain, ln1_bias, w_qkv, w_proj, ln2_gain, ln2_bias, w_fc1, w_fc2, cotangent
):
    row_count = inputs.shape[1]
    model_width = inputs.shape[2]
    head_count = HEADS
    score_scale = 1.0 / math.sqrt(model_width // head_count)
    seq_crops = crops[0]
    seq_len = seq_crops.shape[0]
    key_block = min(1024, seq_len)
    block_count = seq_len // key_block
    block_ids = jnp.arange(block_count)
    own_crops = lax.dynamic_slice_in_dim(seq_crops, lax.axis_index("blk") * row_count, row_count, 0)
    residual = inputs[0].astype(jnp.float32)
    normed_one_low = layer_norm(residual, ln1_gain, ln1_bias).astype(jnp.bfloat16)
    qkv_low = jnp.dot(normed_one_low, w_qkv, preferred_element_type=jnp.float32).astype(
        jnp.bfloat16
    )
    query_own = qkv_low[:, :model_width]
    key_own = qkv_low[:, model_width : 2 * model_width]
    value_own = qkv_low[:, 2 * model_width :]
    keys_all, values_all = (
        lax.all_gather(key_own, "blk", axis=0, tiled=True),
        lax.all_gather(value_own, "blk", axis=0, tiled=True),
    )
    query_heads = head_view(query_own, head_count)

    def block_inputs(block_index):
        key_heads = head_view(
            lax.dynamic_slice_in_dim(keys_all, block_index * key_block, key_block, 0), head_count
        )
        value_heads = head_view(
            lax.dynamic_slice_in_dim(values_all, block_index * key_block, key_block, 0), head_count
        )
        crop_block = lax.dynamic_slice_in_dim(seq_crops, block_index * key_block, key_block, 0)
        visible = own_crops[:, None] == crop_block[None, :]
        return (key_heads, value_heads, visible)

    def stats_step(carried, block_index):
        old_max, summed = carried
        key_heads, value_heads, visible = block_inputs(block_index)
        scores = jnp.where(visible[None], scores_of(query_heads, key_heads, score_scale), MASKED)
        new_max = jnp.maximum(old_max, jnp.max(scores, axis=-1))
        exp_terms = jnp.where(visible[None], jnp.exp(scores - new_max[:, :, None]), 0.0)
        return ((new_max, summed * jnp.exp(old_max - new_max) + jnp.sum(exp_terms, axis=-1)), None)

    start_max = jnp.full((head_count, row_count), MASKED, jnp.float32)
    start_sum = jnp.zeros((head_count, row_count), jnp.float32)
    (row_max, summed), _ = lax.scan(stats_step, (start_max, start_sum), block_ids)
    logsum = row_max + jnp.log(summed)

    def output_step(running, block_index):
        key_heads, value_heads, visible = block_inputs(block_index)
        attn_probs = weights_of(
            scores_of(query_heads, key_heads, score_scale), visible, logsum
        ).astype(jnp.bfloat16)
        return (
            running
            + jnp.einsum(
                "hqk,khd->qhd", attn_probs, value_heads, preferred_element_type=jnp.float32
            ),
            None,
        )

    attended, _ = lax.scan(output_step, jnp.zeros(query_heads.shape, jnp.float32), block_ids)
    attended_low = attended.reshape(row_count, model_width).astype(jnp.bfloat16)
    mixed_rows = residual + jnp.dot(attended_low, w_proj, preferred_element_type=jnp.float32)
    normed_two_low = layer_norm(mixed_rows, ln2_gain, ln2_bias).astype(jnp.bfloat16)
    hidden_pre = jnp.dot(normed_two_low, w_fc1, preferred_element_type=jnp.float32)
    active, gelu_back = jax.vjp(jax.nn.gelu, hidden_pre)
    active_low = active.astype(jnp.bfloat16)
    result = mixed_rows + jnp.dot(active_low, w_fc2, preferred_element_type=jnp.float32)
    output = result.astype(jnp.bfloat16)[None]
    grad_out_low = cotangent[0]
    grad_fc2 = contract_rows(active_low, grad_out_low)
    grad_active = against_weight(grad_out_low, w_fc2)
    grad_hidden_low = gelu_back(grad_active)[0].astype(jnp.bfloat16)
    grad_fc1 = contract_rows(normed_two_low, grad_hidden_low)
    grad_normed_two = against_weight(grad_hidden_low, w_fc1)
    _, norm_two_back = jax.vjp(layer_norm, mixed_rows, ln2_gain, ln2_bias)
    grad_mixed_part, grad_gain_two, grad_bias_two = norm_two_back(grad_normed_two)
    grad_mixed = grad_out_low.astype(jnp.float32) + grad_mixed_part
    grad_mixed_low = grad_mixed.astype(jnp.bfloat16)
    grad_proj = contract_rows(attended_low, grad_mixed_low)
    grad_attended_low = against_weight(grad_mixed_low, w_proj).astype(jnp.bfloat16)
    grad_heads = head_view(grad_attended_low, head_count)

    def delta_step(running, block_index):
        key_heads, value_heads, visible = block_inputs(block_index)
        attn_probs = weights_of(scores_of(query_heads, key_heads, score_scale), visible, logsum)
        grad_probs = jnp.einsum(
            "qhd,khd->hqk", grad_heads, value_heads, preferred_element_type=jnp.float32
        )
        return (running + jnp.sum(attn_probs * grad_probs, axis=-1), None)

    row_delta, _ = lax.scan(delta_step, jnp.zeros((head_count, row_count), jnp.float32), block_ids)

    def score_grads(
        query_part, grad_part, logsum_part, delta_part, key_heads, value_heads, visible
    ):
        attn_probs = weights_of(scores_of(query_part, key_heads, score_scale), visible, logsum_part)
        grad_probs = jnp.einsum(
            "qhd,khd->hqk", grad_part, value_heads, preferred_element_type=jnp.float32
        )
        grad_scores = (attn_probs * (grad_probs - delta_part[:, :, None])).astype(jnp.bfloat16)
        return (attn_probs, grad_scores)

    def pair_step(running, block_index):
        key_heads, value_heads, visible = block_inputs(block_index)
        attn_probs, grad_scores = score_grads(
            query_heads, grad_heads, logsum, row_delta, key_heads, value_heads, visible
        )
        key_term = (
            jnp.einsum("hqk,qhd->khd", grad_scores, query_heads, preferred_element_type=jnp.float32)
            * score_scale
        )
        value_term = jnp.einsum(
            "hqk,qhd->khd",
            attn_probs.astype(jnp.bfloat16),
            grad_heads,
            preferred_element_type=jnp.float32,
        )
        joined = jnp.concatenate(
            [key_term.reshape(key_block, model_width), value_term.reshape(key_block, model_width)],
            axis=1,
        )
        step_query = jnp.einsum(
            "hqk,khd->qhd", grad_scores, key_heads, preferred_element_type=jnp.float32
        )
        return (running + step_query, joined)

    grad_query, key_terms = lax.scan(
        pair_step, jnp.zeros(query_heads.shape, jnp.float32), block_ids
    )
    key_sums = lax.psum_scatter(
        key_terms.reshape(seq_len, 2 * model_width).astype(jnp.bfloat16),
        "blk",
        scatter_dimension=0,
        tiled=True,
    ).astype(jnp.float32)
    grad_key = key_sums[:, :model_width]
    grad_value = key_sums[:, model_width:]
    grad_query = grad_query.reshape(row_count, model_width) * score_scale
    grad_qkv_low = jnp.concatenate([grad_query, grad_key, grad_value], axis=1).astype(jnp.bfloat16)
    grad_wqkv = contract_rows(normed_one_low, grad_qkv_low)
    grad_normed_one = against_weight(grad_qkv_low, w_qkv)
    _, norm_one_back = jax.vjp(layer_norm, residual, ln1_gain, ln1_bias)
    grad_resid, grad_gain_one, grad_bias_one = norm_one_back(grad_normed_one)
    grad_input = (grad_mixed + grad_resid).astype(jnp.bfloat16)[None]
    (
        fc1_share,
        fc2_share,
        qkv_share,
        proj_share,
        gain_one_share,
        bias_one_share,
        gain_two_share,
        bias_two_share,
    ) = (
        lax.psum_scatter(
            grad_fc1.astype(jnp.bfloat16), "blk", scatter_dimension=0, tiled=True
        ).astype(jnp.float32),
        lax.psum_scatter(
            grad_fc2.astype(jnp.bfloat16), "blk", scatter_dimension=0, tiled=True
        ).astype(jnp.float32),
        lax.psum_scatter(
            grad_wqkv.astype(jnp.bfloat16), "blk", scatter_dimension=0, tiled=True
        ).astype(jnp.float32),
        lax.psum_scatter(
            grad_proj.astype(jnp.bfloat16), "blk", scatter_dimension=0, tiled=True
        ).astype(jnp.float32),
        lax.psum_scatter(
            grad_gain_one.astype(jnp.bfloat16), "blk", scatter_dimension=0, tiled=True
        ).astype(jnp.float32),
        lax.psum_scatter(
            grad_bias_one.astype(jnp.bfloat16), "blk", scatter_dimension=0, tiled=True
        ).astype(jnp.float32),
        lax.psum_scatter(
            grad_gain_two.astype(jnp.bfloat16), "blk", scatter_dimension=0, tiled=True
        ).astype(jnp.float32),
        lax.psum_scatter(
            grad_bias_two.astype(jnp.bfloat16), "blk", scatter_dimension=0, tiled=True
        ).astype(jnp.float32),
    )
    totals = (
        lax.psum(qkv_share.astype(jnp.bfloat16), "dp").astype(jnp.float32),
        lax.psum(proj_share.astype(jnp.bfloat16), "dp").astype(jnp.float32),
        lax.psum(fc1_share.astype(jnp.bfloat16), "dp").astype(jnp.float32),
        lax.psum(fc2_share.astype(jnp.bfloat16), "dp").astype(jnp.float32),
        lax.psum(gain_one_share.astype(jnp.bfloat16), "dp").astype(jnp.float32),
        lax.psum(bias_one_share.astype(jnp.bfloat16), "dp").astype(jnp.float32),
        lax.psum(gain_two_share.astype(jnp.bfloat16), "dp").astype(jnp.float32),
        lax.psum(bias_two_share.astype(jnp.bfloat16), "dp").astype(jnp.float32),
    )
    return (
        output,
        grad_input,
        totals[0],
        totals[1],
        totals[2],
        totals[3],
        totals[4],
        totals[5],
        totals[6],
        totals[7],
    )


def solution(mesh):
    placed = (
        P("dp", "blk", None),
        P("dp", None),
        P(),
        P(),
        P(),
        P(),
        P(),
        P(),
        P(),
        P(),
        P("dp", "blk", None),
    )
    return jax.shard_map(
        shards,
        mesh=mesh,
        in_specs=placed,
        out_specs=(
            P("dp", "blk", None),
            P("dp", "blk", None),
            P("blk", None),
            P("blk", None),
            P("blk", None),
            P("blk", None),
            P("blk"),
            P("blk"),
            P("blk"),
            P("blk"),
        ),
        check_vma=False,
    )
```

profile of v0, /device:TPU:0, one launch (start us, length us, event | category | flops | bytes accessed | tf_op | source)
XLA Modules:
  0.0 460.3 jit_solution(4675671645990532196)
XLA Ops:
  7.2 1.2 convert_reduce_fusion
  10.1 1.6 convolution_convert_fusion.3
  13.4 1.7 copy.34
  16.0 25.2 %all-gather.5.cloned.1.call-done = bf16[1024,768]{1,0:T(8,128)(2,1)} async-done(((bf16[128,768]{1,0:T(8,128)(2,1)}), bf16[1024,768]{1,0:T(8,128)(2,1)}) %all-gather.5.cloned.1.call-update) | async-done | bytes 1572880 | tf_op jit(solution)/shard_map/all_gather | solution.py:71
  41.2 2.6 copy.35
  43.7 2.7 select_reduce_fusion.1
  46.5 2.0 select_reduce_fusion
  49.2 20.2 %all-gather.3.cloned.1.call-done = bf16[1024,768]{1,0:T(8,128)(2,1)} async-done(((bf16[128,768]{1,0:T(8,128)(2,1)}), bf16[1024,768]{1,0:T(8,128)(2,1)}) %all-gather.3.cloned.1.call-update) | async-done | bytes 1572880 | tf_op jit(solution)/shard_map/all_gather | solution.py:72
  69.3 2.6 copy.33
  71.9 4.8 %convolution_convert_fusion.7 = bf16[12,64,128]{2,1,0:T(8,128)(2,1)S(1)} fusion(bf16[1024,12,64]{0,2,1:T(8,128)(2,1)} %bitcast.101, f32[12,128,1024]{2,1,0:T(8,128)} %copy-done.1, f32[12,128]{1,0:T(8,128)S(1)} %log_add_fusion, pred[128,1024]{1,0:T(8,128)(4,1)} %broadcast_compare_fusion), kind=kOutput, calls=%fused_computation.30 | convolution fusion | flops 207716352 | bytes 8198144 | tf_op jit(solution)/shard_map/while/body/eval_jaxpr/hqk,khd->qhd/dot_general | solution.py:107
  77.5 3.3 fusion.44
  80.9 4.8 %fusion.7 = bf16[128,3072]{1,0:T(8,128)(2,1)S(1)} fusion(f32[128,3072]{1,0:T(8,128)S(1)} %fusion.44, bf16[3072,768]{1,0:T(8,128)(2,1)} %param.20, bf16[1,128,768]{2,1,0:T(8,128)(2,1)S(1)} %copy-done.15), kind=kOutput, calls=%fused_computation.21 | convolution fusion | flops 611844096 | bytes 7274496 | tf_op jit(solution)/shard_map/dot_general | solution.py:29
  85.7 2.3 multiply_reduce_fusion.1
  89.9 1.2 convolution_convert_fusion.6
  91.1 1.7 copy.36
  92.8 4.5 convolution_convert_fusion.4
  97.4 4.8 %multiply_reduce_fusion = (f32[12,128]{1,0:T(8,128)S(1)}, f32[12,128,1024]{2,1,0:T(8,128)S(1)}) fusion(f32[12,128,1024]{2,1,0:T(8,128)} %copy-done.1, f32[12,128]{1,0:T(8,128)S(1)} %log_add_fusion, pred[128,1024]{1,0:T(8,128)(4,1)S(1)} %copy-done.11, bf16[128,12,64]{0,2,1:T(8,128)(2,1)S(1)} %bitcast.107, bf16[1024,12,64]{0,2,1:T(8,128)(2,1)S(1)} %bitcast.102), kind=kOutput, calls=%fused_computation.1 | convolution fusion | flops 209189376 | bytes 14495744 | tf_op jit(solution)/shard_map/while/body/eval_jaxpr/qhd,khd->hqk/dot_general | solution.py:150
  102.2 2.3 multiply_convert_fusion
  104.4 1.7 copy-done.2
  106.7 2.0 pad_maximum_fusion
  108.6 4.7 %copy.37 = bf16[1024,1536]{1,0:T(8,128)(2,1)} copy(bf16[1024,1536]{0,1:T(8,128)(2,1)} %pad_maximum_fusion) | data formatting | bytes 6291456
  113.4 2.5 convolution_convert_fusion.5
  116.0 5.2 %convolution_convert_fusion = bf16[3072,768]{1,0:T(8,128)(2,1)} fusion(bf16[1,128,768]{2,1,0:T(8,128)(2,1)} %param.21, f32[128,3072]{1,0:T(8,128)} %copy-done.4), kind=kOutput, calls=%fused_computation.5 | convolution fusion | flops 609878016 | bytes 6488064 | tf_op jit(solution)/shard_map/dot_general | solution.py:23
  121.9 5.0 %convolution_convert_fusion.1 = bf16[768,3072]{1,0:T(8,128)(2,1)} fusion(bf16[128,3072]{1,0:T(8,128)(2,1)} %copy-done.12, f32[128,768]{1,0:T(8,128)} %copy-done.3, f32[768]{0:T(1024)S(1)} %copy-done.23, f32[768]{0:T(1024)S(1)} %copy-done.22, f32[128]{0:T(128)S(1)} %copy-done.31, f32[128]{0:T(128)S(1)} %copy-done.26), kind=kOutput, calls=%fused_computation.6 | convolution fusion | flops 606830592 | bytes 5905408 | tf_op jit(solution)/shard_map/dot_general | solution.py:23
  127.0 4.3 fusion.9
  131.2 28.5 %reduce-scatter.16.cloned.1.call-done = bf16[128,1536]{1,0:T(8,128)(2,1)} async-done(((bf16[1024,1536]{1,0:T(8,128)(2,1)}), bf16[128,1536]{1,0:T(8,128)(2,1)}) %reduce-scatter.16.cloned.1.call-update) | async-done | bytes 393232
  159.8 1.9 copy.38
  161.7 4.2 convolution_convert_fusion.2
  166.0 34.6 %reduce-scatter.10.cloned.1.call-done = bf16[96,768]{1,0:T(8,128)(2,1)} async-done(((bf16[768,768]{1,0:T(8,128)(2,1)}), bf16[96,768]{1,0:T(8,128)(2,1)}) %reduce-scatter.10.cloned.1.call-update) | async-done | bytes 147472 | tf_op jit(solution)/shard_map/reduce_scatter | solution.py:217
  200.6 57.2 %reduce-scatter.14.cloned.1.call-done = bf16[384,768]{1,0:T(8,128)(2,1)} async-done(((bf16[3072,768]{1,0:T(8,128)(2,1)}), bf16[384,768]{1,0:T(8,128)(2,1)}) %reduce-scatter.14.cloned.1.call-update) | async-done | bytes 589840 | tf_op jit(solution)/shard_map/reduce_scatter | solution.py:211
  257.7 57.6 %reduce-scatter.12.cloned.1.call-done = bf16[96,3072]{1,0:T(8,128)(2,1)} async-done(((bf16[768,3072]{1,0:T(8,128)(2,1)}), bf16[96,3072]{1,0:T(8,128)(2,1)}) %reduce-scatter.12.cloned.1.call-update) | async-done | bytes 589840 | tf_op jit(solution)/shard_map/reduce_scatter | solution.py:208
  315.3 51.6 %reduce-scatter.8.cloned.1.call-done = bf16[96,2304]{1,0:T(8,128)(2,1)} async-done(((bf16[768,2304]{1,0:T(8,128)(2,1)}), bf16[96,2304]{1,0:T(8,128)(2,1)}) %reduce-scatter.8.cloned.1.call-update) | async-done | bytes 442384 | tf_op jit(solution)/shard_map/reduce_scatter | solution.py:214
  368.3 4.7 %fusion.10 = bf16[1,128,768]{2,1,0:T(8,128)(2,1)} fusion(f32[128,768]{1,0:T(8,128)} %copy-done.3, bf16[3072,768]{1,0:T(8,128)(2,1)} %param.20, f32[128,3072]{1,0:T(8,128)} %copy-done.4), kind=kOutput, calls=%fused_computation.31 | convolution fusion | flops 607715328 | bytes 6881280 | tf_op jit(solution)/shard_map/dot_general | solution.py:120
  373.0 1.9 fusion.45
  375.7 14.5 %all-reduce.4 = (bf16[768]{0:T(1024)(128)(2,1)}, bf16[768]{0:T(1024)(128)(2,1)}, bf16[768]{0:T(1024)(128)(2,1)}, bf16[768]{0:T(1024)(128)(2,1)}) all-reduce(bf16[768]{0:T(1024)(128)(2,1)} %get-tuple-element.86, bf16[768]{0:T(1024)(128)(2,1)} %get-tuple-element.98, ...), channel_id=7, replica_groups=mesh['dp'=4,'blk'=8] {'blk'}, use_global_device_ids=true, to_apply=%region_21.22.clone | all-reduce | flops 3072 | bytes 12288
  391.0 1.3 dynamic-slice.4
  392.2 1.3 dynamic-slice.6
  393.5 1.3 dynamic-slice.8
  394.8 12.9 %all-reduce.5 = (bf16[96]{0:T(256)(128)(2,1)}, bf16[96]{0:T(256)(128)(2,1)}, bf16[96]{0:T(256)(128)(2,1)}, bf16[96]{0:T(256)(128)(2,1)}) all-reduce(bf16[96]{0:T(256)(128)(2,1)S(1)} %dynamic-slice.2, bf16[96]{0:T(256)(128)(2,1)} %dynamic-slice.4, bf16[96]{0:T(256)(128)(2,1)} %dynamic-slice.6, ...), channel_id=1, replica_groups=mesh['dp'=4,'blk'=8] {'dp'}, use_global_device_ids=true, to_apply=%region_22.23 | all-reduce | flops 384 | bytes 1536 | tf_op jit(solution)/shard_map/psum | solution.py:238
  407.7 1.2 convert_element_type.148
  408.9 1.2 convert_element_type.150
  410.1 1.2 convert_element_type.152
  411.2 1.2 convert_element_type.154
  413.0 2.3 fusion.25
  415.3 31.2 %all-reduce.9.cloned.1.call-done = (bf16[96,2304]{1,0:T(8,128)(2,1)}, bf16[96,768]{1,0:T(8,128)(2,1)}, bf16[96,3072]{1,0:T(8,128)(2,1)}, bf16[384,768]{1,0:T(8,128)(2,1)}) async-done(((bf16[96,2304]{1,0:T(8,128)(2,1)}, bf16[96,768]{1,0:T(8,128)(2,1)}, bf16[96,3072]{1,0:T(8,128)(2,1)}, bf16[384,768]{1,0:T(8,128)(2,1)}), (bf16[96,2304]{1,0:T(8,128)(2,1)}, bf16[96,768]{1,0:T(8,128)(2,1)}, ...) | async-done | bytes 1769488 | tf_op jit(solution)/shard_map/psum | solution.py:234
  446.5 1.7 convert_element_type.142
  448.2 2.0 convert_element_type.140
  450.2 2.2 convert_element_type.144
  (130 shorter events, 12.6 us)
Async XLA Ops:
  7.2 2.9 copy-start
  7.2 34.0 %all-gather.5.cloned.1.call-start = ((), (), s32[]{:S(2)}) async-start(), calls=%async_computation.6 | async-start | bytes 1769472 | tf_op jit(solution)/shard_map/all_gather | solution.py:71
  8.4 4.1 copy-start.28
  10.1 2.5 copy-start.32
  10.1 5.1 %copy-start.35 = (s32[1,1024]{1,0:T(1,128)S(1)}, s32[1,1024]{1,0:T(1,128)}, u32[]{:S(2)}) copy-start(s32[1,1024]{1,0:T(1,128)} %param.12) | copy-start | bytes 12292
  12.6 56.7 %all-gather.3.cloned.1.call-start = ((), (), s32[]{:S(2)}) async-start(), calls=%async_computation.5 | async-start | bytes 1769472 | tf_op jit(solution)/shard_map/all_gather | solution.py:72
  13.4 146.4 %reduce-scatter.16.cloned.1.call-start = ((), (), s32[]{:S(2)}) async-start(), calls=%async_computation.11 | async-start | bytes 3538944
  43.7 2.8 copy-start.10
  46.5 2.7 copy-start.1
  71.9 4.8 %copy-start.5 = (bf16[1,128,768]{2,1,0:T(8,128)(2,1)S(1)}, bf16[1,128,768]{2,1,0:T(8,128)(2,1)}, u32[]{:S(2)}) copy-start(bf16[1,128,768]{2,1,0:T(8,128)(2,1)} %param.11) | copy-start | bytes 589828
  71.9 4.8 %copy-start.8 = (bf16[768,768]{1,0:T(8,128)(2,1)S(1)}, bf16[768,768]{1,0:T(8,128)(2,1)}, u32[]{:S(2)}) copy-start(bf16[768,768]{1,0:T(8,128)(2,1)} %param.16) | copy-start | bytes 3538948
  71.9 5.5 %copy-start.22 = (f32[768]{0:T(1024)S(1)}, f32[768]{0:T(1024)}, u32[]{:S(2)}) copy-start(f32[768]{0:T(1024)} %param.17) | copy-start | bytes 9220
  71.9 5.5 %copy-start.23 = (f32[768]{0:T(1024)S(1)}, f32[768]{0:T(1024)}, u32[]{:S(2)}) copy-start(f32[768]{0:T(1024)} %param.18) | copy-start | bytes 9220
  77.2 10.8 %copy-start.3 = (f32[128,768]{1,0:T(8,128)}, f32[128,768]{1,0:T(8,128)S(1)}, u32[]{:S(2)}) copy-start(f32[128,768]{1,0:T(8,128)S(1)} %get-tuple-element.142) | copy-start | bytes 1179652
  77.2 10.8 %copy-start.25 = (f32[128]{0:T(128)}, f32[128]{0:T(128)S(1)}, u32[]{:S(2)}) copy-start(f32[128]{0:T(128)S(1)} %broadcast_multiply_fusion) | copy-start | bytes 1540
  77.5 10.6 %copy-start.30 = (f32[128]{0:T(128)}, f32[128]{0:T(128)S(1)}, u32[]{:S(2)}) copy-start(f32[128]{0:T(128)S(1)} %fusion.34) | copy-start | bytes 1540
  77.5 3.4 copy-start.15
  77.5 8.2 %slice-start.2 = ((s8[4718592]{0:T(1024)(128)(4,1)}), s8[4194304]{0:T(1024)(128)(4,1)S(1)}, s32[]{:S(2)}) async-start(s8[4718592]{0:T(1024)(128)(4,1)} %bitcast.96), calls=%async_computation.15 | async-start | bytes 8388608
  80.9 4.8 %copy-start.4 = (f32[128,3072]{1,0:T(8,128)}, f32[128,3072]{1,0:T(8,128)S(1)}, u32[]{:S(2)}) copy-start(f32[128,3072]{1,0:T(8,128)S(1)} %fusion.44) | copy-start | bytes 4718596
  80.9 4.8 %slice-start.3 = ((s8[4718592]{0:T(1024)(128)(4,1)}), s8[524288]{0:T(1024)(128)(4,1)S(1)}, s32[]{:S(2)}) async-start(s8[4718592]{0:T(1024)(128)(4,1)} %bitcast.96), calls=%async_computation.16 | async-start | bytes 1048576
  85.7 2.3 copy-start.12
  88.3 0.7 copy-start.9
  88.3 0.9 copy-start.37
  92.8 4.5 copy-start.7
  92.8 4.5 copy-start.11
  92.8 4.5 copy-start.18
  92.8 9.3 %slice-start = ((s8[6291456]{0:T(1024)(128)(4,1)}), s8[4194304]{0:T(1024)(128)(4,1)S(1)}, s32[]{:S(2)}) async-start(s8[6291456]{0:T(1024)(128)(4,1)} %bitcast.94), calls=%async_computation.13 | async-start | bytes 8388608
  97.4 4.8 %slice-start.1 = ((s8[6291456]{0:T(1024)(128)(4,1)}), s8[2097152]{0:T(1024)(128)(4,1)S(1)}, s32[]{:S(2)}) async-start(s8[6291456]{0:T(1024)(128)(4,1)} %bitcast.94), calls=%async_computation.14 | async-start | bytes 4194304
  102.2 3.9 copy-start.13
  104.4 1.7 copy-start.2
  113.4 87.2 %reduce-scatter.10.cloned.1.call-start = ((), (), s32[]{:S(2)}) async-start(), calls=%async_computation.8 | async-start | bytes 1327104 | tf_op jit(solution)/shard_map/reduce_scatter | solution.py:217
  116.0 141.8 %reduce-scatter.14.cloned.1.call-start = ((), (), s32[]{:S(2)}) async-start(), calls=%async_computation.10 | async-start | bytes 5308416 | tf_op jit(solution)/shard_map/reduce_scatter | solution.py:211
  121.2 194.1 %reduce-scatter.12.cloned.1.call-start = ((), (), s32[]{:S(2)}) async-start(), calls=%async_computation.9 | async-start | bytes 5308416 | tf_op jit(solution)/shard_map/reduce_scatter | solution.py:208
  126.9 34.8 %copy-start.24 = (f32[768]{0:T(1024)S(1)}, f32[768]{0:T(1024)}, u32[]{:S(2)}) copy-start(f32[768]{0:T(1024)} %param.13) | copy-start | bytes 9220
  126.9 34.8 %copy-start.27 = (f32[768]{0:T(1024)S(1)}, f32[768]{0:T(1024)}, u32[]{:S(2)}) copy-start(f32[768]{0:T(1024)} %param.14) | copy-start | bytes 9220
  126.9 34.8 %copy-start.29 = (f32[128]{0:T(128)S(1)}, f32[128]{0:T(128)}, u32[]{:S(2)}) copy-start(f32[128]{0:T(128)} %copy-done.28) | copy-start | bytes 1540
  126.9 34.8 %copy-start.33 = (f32[128]{0:T(128)S(1)}, f32[128]{0:T(128)}, u32[]{:S(2)}) copy-start(f32[128]{0:T(128)} %copy-done.32) | copy-start | bytes 1540
  126.9 240.0 %reduce-scatter.8.cloned.1.call-start = ((), (), s32[]{:S(2)}) async-start(), calls=%async_computation.7 | async-start | bytes 3981312 | tf_op jit(solution)/shard_map/reduce_scatter | solution.py:214
  165.9 201.1 %copy-start.40 = (u32[32]{0:T(128)S(1)}, u32[32]{0:T(128)}, u32[]{:S(2)}) copy-start(u32[32]{0:T(128)} %constant.111) | copy-start | bytes 388
  165.9 280.6 %all-reduce.9.cloned.1.call-start = ((), (), s32[]{:S(2)}) async-start(), calls=%async_computation.12 | async-start | bytes 3538944 | tf_op jit(solution)/shard_map/psum | solution.py:234
  368.2 4.7 %copy-start.6 = (bf16[1,128,768]{2,1,0:T(8,128)(2,1)S(1)}, bf16[1,128,768]{2,1,0:T(8,128)(2,1)}, u32[]{:S(2)}) copy-start(bf16[1,128,768]{2,1,0:T(8,128)(2,1)} %param.11) | copy-start | bytes 589828
  368.3 4.7 %copy-start.16 = (bf16[128,1536]{0,1:T(8,128)(2,1)S(1)}, bf16[128,1536]{0,1:T(8,128)(2,1)}, u32[]{:S(2)}) copy-start(bf16[128,1536]{0,1:T(8,128)(2,1)} %copy.38) | copy-start | bytes 1179652
  368.3 4.7 %copy-start.19 = (bf16[12,64,128]{2,1,0:T(8,128)(2,1)S(1)}, bf16[12,64,128]{2,1,0:T(8,128)(2,1)}, u32[]{:S(2)}) copy-start(bf16[12,64,128]{2,1,0:T(8,128)(2,1)} %fusion.9) | copy-start | bytes 589828
  373.0 2.0 copy-start.39
  373.0 2.8 copy-start.34
  374.9 0.8 copy-start.17
  374.9 0.8 copy-start.36
  446.5 5.9 %copy-start.21 = (bf16[384,768]{1,0:T(8,128)(2,1)S(1)}, bf16[384,768]{1,0:T(8,128)(2,1)}, u32[]{:S(2)}) copy-start(bf16[384,768]{1,0:T(8,128)(2,1)} %get-tuple-element.122) | copy-start | bytes 1769476
  (5 other events, 3.1 us)
Sparse Core Ops, SparseCore 0:
  12.7 28.3 all-gather.4
  43.6 25.6 all-gather.2
  113.5 46.2 reduce-scatter.15
  163.8 36.7 reduce-scatter.9
  203.8 53.8 reduce-scatter.13
  261.4 53.8 reduce-scatter.11
  318.8 48.0 reduce-scatter.7
  369.6 76.8 all-reduce.8
where the time goes:
time: 461 us; the launch traced here: 460 us
  waiting for transfers between devices  307 us (67%)
  matrix products  58.8 us (13%)
  blocking collectives  27.4 us (6%)
  local copies, waits for them, and re-layouts  26.2 us (6%)
  other arithmetic  25.2 us (5%)
  between operations  15.4 us (3%)
    reduce_scatter x1, waiting for transfers between devices, shards(): lax.psum_scatter(grad_fc1.astype(jnp.bfloat16), 'blk', scatter_dimension=...  57.6 us
    reduce_scatter x1, waiting for transfers between devices, shards(): lax.psum_scatter(grad_fc2.astype(jnp.bfloat16), 'blk', scatter_dimension=...  57.2 us
    reduce_scatter x1, waiting for transfers between devices, shards(): lax.psum_scatter(grad_wqkv.astype(jnp.bfloat16), 'blk', scatter_dimension...  51.6 us
    reduce_scatter x1, waiting for transfers between devices, shards(): lax.psum_scatter(grad_proj.astype(jnp.bfloat16), 'blk', scatter_dimension...  34.6 us
    psum x1, waiting for transfers between devices, shards(): lax.psum(qkv_share.astype(jnp.bfloat16), 'dp').astype(jnp.float32)  31.2 us
    unnamed x9, waiting for transfers between devices  29.4 us
    all_gather x1, waiting for transfers between devices, shards(): lax.all_gather(key_own, 'blk', axis=0, tiled=True)  25.2 us
    all_gather x1, waiting for transfers between devices, shards(): lax.all_gather(value_own, 'blk', axis=0, tiled=True)  20.2 us
  transfers between devices with their start and end apart: 8, of which 8 were waited for; matrix products, arithmetic and copies ran while one was open for 12% of the time, Pallas kernels for 0%

commit v1 on v0

--- a/solution.py
+++ b/solution.py
@@ -1,8 +1,11 @@
+import functools
 import math
 
 import jax
 import jax.numpy as jnp
 from jax import lax
+from jax.experimental import pallas as pl
+from jax.experimental.pallas import tpu as pltpu
 from jax.sharding import PartitionSpec as P
 
 HEADS = 12
@@ -254,6 +257,686 @@
     )
 
 
+MESH = pl.DeviceIdType.MESH
+F32 = jnp.float32
+BF16 = jnp.bfloat16
+RUN_ROWS = 128
+HEAD = 64
+
+
+def mm(left, right):
+    return lax.dot_general(left, right, (((1,), (0,)), ((), ())), preferred_element_type=F32)
+
+
+def mm_nt(left, right):
+    return lax.dot_general(left, right, (((1,), (1,)), ((), ())), preferred_element_type=F32)
+
+
+def mm_tn(left, right):
+    return lax.dot_general(left, right, (((0,), (0,)), ((), ())), preferred_element_type=F32)
+
+
+def norm_parts(rows):
+    centred = rows - jnp.mean(rows, axis=-1, keepdims=True)
+    inv_std = lax.rsqrt(jnp.mean(centred * centred, axis=-1, keepdims=True) + EPSILON)
+    return centred * inv_std, inv_std
+
+
+def norm_back(grad_rows, hat, inv_std, gain):
+    grad_hat = grad_rows * gain
+    return inv_std * (
+        grad_hat
+        - jnp.mean(grad_hat, axis=-1, keepdims=True)
+        - hat * jnp.mean(grad_hat * hat, axis=-1, keepdims=True)
+    )
+
+
+def gelu_pair(u):
+    inner = 0.7978845608028654 * (u + 0.044715 * u * u * u)
+    t = jnp.tanh(inner)
+    half = 0.5 * (1.0 + t)
+    slope = half + 0.5 * u * (1.0 - t * t) * (0.7978845608028654 * (1.0 + 0.134145 * u * u))
+    return u * half, slope
+
+
+def layer_kernel(Z, names, *refs):
+    r = dict(zip(names, refs, strict=True))
+    z = lax.axis_index("dp")
+    b = lax.axis_index("blk")
+    e = lax.rem(b, 2)
+    chip = b // 2
+    cx = lax.rem(chip, 2)
+    cy = chip // 2
+    scale = HEAD**-0.5
+
+    def chip_at(delta):
+        dx, dy = delta % 2, delta // 2
+        return 2 * (cy + dy - 2 * cy * dy) + (cx + dx - 2 * cx * dx)
+
+    def dev(delta):
+        return (z, 2 * chip_at(delta) + e)
+
+    other = (z, b + 1 - 2 * e)
+    slot_other = b + 1 - 2 * e
+
+    def remote(src, dst, send_sem, recv_sem, device):
+        return pltpu.make_async_remote_copy(
+            src_ref=src, dst_ref=dst, send_sem=send_sem, recv_sem=recv_sem,
+            device_id=device, device_id_type=MESH,
+        )
+
+    loads = []
+
+    def load(src, dst, at):
+        copy = pltpu.make_async_copy(src, dst, r["ld_sem"].at[at])
+        copy.start()
+        loads.append(copy)
+
+    load(r["x"], r["xb"].at[b], 0)
+    for t in range(3):
+        first = pl.multiple_of(768 * t + 384 * e, 128)
+        load(r["w_qkv"].at[:, pl.ds(first, 384)], r["wf"].at[:, pl.ds(384 * t, 384)], 1 + t)
+    load(r["w_proj"], r["wp"], 4)
+    load(r["w_fc1"].at[:, pl.ds(pl.multiple_of(384 * b, 128), 384)], r["w1"], 5)
+    load(r["w_fc2"].at[pl.ds(pl.multiple_of(384 * b, 128), 384)], r["w2"], 6)
+    load(r["dy"], r["dyb"].at[b], 7)
+    for t in range(3):
+        first = pl.multiple_of(768 * t + 192 * chip - 64 * lax.rem(chip, 2), 128)
+        load(r["w_qkv"].at[:, pl.ds(first, 256)], r["w4"].at[t], 8 + t)
+
+    bar = pltpu.get_barrier_semaphore()
+    for target in (other, dev(1), dev(2), dev(3)):
+        pl.semaphore_signal(bar, inc=1, device_id=target, device_id_type=MESH)
+
+    @pl.when(z > 0)
+    def _():
+        pl.semaphore_signal(bar, inc=1, device_id=(z - 1, b), device_id_type=MESH)
+
+    @pl.when(z < Z - 1)
+    def _():
+        pl.semaphore_signal(bar, inc=1, device_id=(z + 1, b), device_id_type=MESH)
+
+    pl.semaphore_wait(bar, 4 + jnp.minimum(z, 1) + jnp.minimum(Z - 1 - z, 1))
+
+    class Gather:
+        def __init__(self, buf, ss, rs):
+            self.buf, self.ss, self.rs = buf, ss, rs
+
+        def to_chip(self, delta, src):
+            return remote(src, self.buf.at[b], self.ss.at[2 * delta], self.rs.at[2 * delta], dev(delta))
+
+        def to_core(self, src):
+            return remote(src, self.buf.at[b], self.ss.at[1], self.rs.at[1], other)
+
+        def slot(self, m):
+            return 2 * chip_at(m // 2) + (e if m % 2 == 0 else 1 - e)
+
+        def send(self, src):
+            for delta in (3, 2, 1):
+                self.to_chip(delta, src).start()
+            self.to_core(src).start()
+
+        def forward(self, delta):
+            at = self.slot(2 * delta)
+            return remote(
+                self.buf.at[at], self.buf.at[at], self.ss.at[2 * delta + 1],
+                self.rs.at[2 * delta + 1], other,
+            )
+
+        def wait_chip(self, delta):
+            at = self.slot(2 * delta)
+            remote(self.buf.at[at], self.buf.at[at], self.ss.at[2 * delta], self.rs.at[2 * delta], dev(delta)).wait_recv()
+            self.forward(delta).start()
+
+        def wait_core(self, delta):
+            at = self.slot(2 * delta + 1)
+            remote(self.buf.at[at], self.buf.at[at], self.ss.at[2 * delta + 1], self.rs.at[2 * delta + 1], other).wait_recv()
+
+        def finish(self, src):
+            for delta in (1, 2, 3):
+                self.to_chip(delta, src).wait_send()
+                self.forward(delta).wait_send()
+            self.to_core(src).wait_send()
+
+    gx = Gather(r["xb"], r["gx_s"], r["gx_r"])
+    gdy = Gather(r["dyb"], r["gdy_s"], r["gdy_r"])
+    gdx = Gather(r["dxb"], r["gdx_s"], r["gdx_r"])
+    gdo = Gather(r["dob"], r["gdo_s"], r["gdo_r"])
+
+    class Chain:
+        def __init__(self, name, K, dtype, sink):
+            self.K, self.dtype, self.sink = K, dtype, sink
+            for part in ("own", "rl", "rr", "tu", "td", "su", "sd", "ru", "rd"):
+                setattr(self, part, r[name + "_" + part])
+
+        def up(self, src, k):
+            return remote(src, self.rl.at[k], self.su.at[k], self.ru.at[k], (z + 1, b))
+
+        def down(self, src, k):
+            return remote(src, self.rr.at[k], self.sd.at[k], self.rd.at[k], (z - 1, b))
+
+        def prime(self, k):
+            if Z == 1:
+                return
+
+            @pl.when(z == 0)
+            def _():
+                self.up(self.own.at[k], k).start()
+
+            @pl.when(z == Z - 1)
+            def _():
+                self.down(self.own.at[k], k).start()
+
+        def tick(self, i):
+            ku = i - z
+
+            @pl.when((z > 0) & (ku >= 0) & (ku < self.K))
+            def _():
+                self.up(self.own.at[ku], ku).wait_recv()
+
+                @pl.when(z < Z - 1)
+                def _():
+                    self.tu[ku] = (self.own[ku].astype(F32) + self.rl[ku].astype(F32)).astype(self.dtype)
+                    self.up(self.tu.at[ku], ku).start()
+
+            kd = i - (Z - 1 - z)
+
+            @pl.when((z < Z - 1) & (kd >= 0) & (kd < self.K))
+            def _():
+                self.down(self.own.at[kd], kd).wait_recv()
+
+                @pl.when(z > 0)
+                def _():
+                    self.td[kd] = (self.own[kd].astype(F32) + self.rr[kd].astype(F32)).astype(self.dtype)
+                    self.down(self.td.at[kd], kd).start()
+
+            k = i - (Z - 1)
+            if 0 <= k < self.K:
+
+                @pl.when(z == 0)
+                def _():
+                    self.sink(k, self.own[k].astype(F32) + self.rr[k].astype(F32))
+
+                @pl.when(z == Z - 1)
+                def _():
+                    self.sink(k, self.own[k].astype(F32) + self.rl[k].astype(F32))
+
+                @pl.when((z > 0) & (z < Z - 1))
+                def _():
+                    self.sink(
+                        k,
+                        self.own[k].astype(F32) + self.rl[k].astype(F32) + self.rr[k].astype(F32),
+                    )
+
+        def finish(self):
+            @pl.when(z < Z - 1)
+            def _():
+                for k in range(self.K):
+                    self.up(self.own.at[k], k).wait_send()
+
+            @pl.when(z > 0)
+            def _():
+                for k in range(self.K):
+                    self.down(self.own.at[k], k).wait_send()
+
+    def sink_a(k, total):
+        low = total.astype(BF16)
+        if k < 4:
+            r["o_fc2"][96 * k : 96 * k + 96, 0:384] = low[0]
+            r["o_fc2"][96 * k : 96 * k + 96, 384:768] = low[1]
+        elif k < 8:
+            src = chip_at(k - 4)
+            r["o_fc1"][:, pl.ds(pl.multiple_of(768 * src, 128), 384)] = low[0]
+            r["o_fc1"][:, pl.ds(pl.multiple_of(768 * src + 384, 128), 384)] = low[1]
+        else:
+            r["o_proj"][:, 0:384] = low[0]
+            r["o_proj"][:, 384:768] = low[1]
+
+    def sink_b(k, total):
+        r["o_qkv"][chip_at(k)] = total.astype(BF16)
+
+    def sink_c(k, total):
+        r["o_ln"][...] = total
+
+    ca = Chain("ca", 9, BF16, sink_a)
+    cb = Chain("cb", 4, BF16, sink_b)
+    cc = Chain("cc", 1, F32, sink_c)
+
+    class Scatter:
+        def __init__(self, name):
+            for part in ("ctx", "crx", "keep", "tx", "rx", "cs", "cr", "ss", "sr"):
+                setattr(self, part, r[name + "_" + part])
+
+        def core(self, j):
+            return remote(self.ctx.at[j], self.crx.at[j], self.cs.at[j], self.cr.at[j], other)
+
+        def send(self, j):
+            delta = 3 - j
+            return remote(self.tx.at[j], self.rx.at[j], self.ss.at[j], self.sr.at[j], dev(delta))
+
+        def put(self, j, mine, theirs):
+            self.keep[j] = mine
+            self.ctx[j] = theirs.astype(BF16)
+            self.core(j).start()
+
+        def sum_core(self, j):
+            self.core(j).wait_recv()
+            return self.keep[j] + self.crx[j].astype(F32)
+
+        def result(self):
+            total = self.sum_core(3)
+            for j in range(3):
+                self.send(j).wait_recv()
+                total += self.rx[j].astype(F32)
+            return total
+
+        def finish(self):
+            for j in range(4):
+                self.core(j).wait_send()
+            for j in range(3):
+                self.send(j).wait_send()
+
+    dn = Scatter("dn")
+    ys = Scatter("ys")
+
+    gx.send(r["x"])
+
+    crop = [r["crops"][0, RUN_ROWS * i] for i in range(8)]
+    places = []
+    for i in range(8):
+        place = 2 * crop[i]
+        for h in range(i):
+            place = place + jnp.where(crop[h] == crop[i], 1, 0)
+        places.append(place)
+        r["inv"][i] = place
+    for s in range(8):
+        run = jnp.int32(0)
+        for i in range(8):
+            run = run + jnp.where(places[i] == s, i, 0)
+        r["perm"][s] = run
+
+    for copy in loads[:4]:
+        copy.wait()
+    for copy in loads[8:]:
+        copy.wait()
+    odd = lax.rem(chip, 2) == 1
+    for t in range(3):
+        r["wo"][:, 192 * t : 192 * t + 192] = jnp.where(odd, r["w4"][t, :, 64:256], r["w4"][t, :, 0:192])
+
+    g1, b1 = r["ln1_gain"][...], r["ln1_bias"][...]
+    g2, b2 = r["ln2_gain"][...], r["ln2_bias"][...]
+
+    for delta in range(4):
+        if delta > 0:
+            gx.wait_chip(delta)
+            gdy.to_chip(delta, r["dy"]).start()
+        else:
+            gdy.to_core(r["dy"]).start()
+        gx.wait_core(delta)
+        pair = pl.ds(2 * chip_at(delta), 2)
+        hat, _ = norm_parts(r["xb"][pair].reshape(256, 768).astype(F32))
+        normed = (hat * g1 + b1).astype(BF16)
+        r["n1"][pair] = normed.reshape(2, 128, 768)
+        r["qkv"][pair] = mm(normed, r["wf"][...]).astype(BF16).reshape(2, 128, 1152)
+
+    def o_core(at):
+        return remote(r["ob"].at[e, pl.ds(2 * at, 2)], r["ob"].at[e, pl.ds(2 * at, 2)], r["o_s"].at[at], r["o_r"].at[at], other)
+
+    def attend(at, carry):
+        run0, run1 = r["perm"][2 * at], r["perm"][2 * at + 1]
+        rows = jnp.concatenate([r["qkv"][run0], r["qkv"][run1]], axis=0)
+        outs = []
+        for h in range(6):
+            q = rows[:, 64 * h : 64 * h + 64]
+            k = rows[:, 384 + 64 * h : 384 + 64 * h + 64]
+            v = rows[:, 768 + 64 * h : 768 + 64 * h + 64]
+            s = mm_nt(q, k) * scale
+            p = jnp.exp(s - jnp.max(s, axis=-1, keepdims=True))
+            p = (p / jnp.sum(p, axis=-1, keepdims=True)).astype(BF16)
+            outs.append(mm(p, v))
+        low = jnp.concatenate(outs, axis=1).astype(BF16)
+        r["ob"][e, pl.ds(2 * at, 2)] = low.reshape(2, 128, 384)
+        o_core(at).start()
+        return carry
+
+    lax.fori_loop(0, 4, attend, 0)
+
+    for delta in (1, 2, 3):
+        gdy.wait_chip(delta)
+    for delta in range(4):
+        gdy.wait_core(delta)
+    for copy in loads[4:8]:
+        copy.wait()
+    for at in range(4):
+        remote(r["ob"].at[1 - e, pl.ds(2 * at, 2)], r["ob"].at[1 - e, pl.ds(2 * at, 2)], r["o_s"].at[at], r["o_r"].at[at], other).wait_recv()
+
+    def o_rows(run):
+        at = r["inv"][run]
+        return jnp.concatenate([r["ob"][0, at], r["ob"][1, at]], axis=1)
+
+    def feed(j, carry):
+        delta = 3 - j
+        c = chip_at(delta)
+        pair = pl.ds(2 * c, 2)
+        o = jnp.concatenate([o_rows(2 * c), o_rows(2 * c + 1)], axis=0)
+        x1 = r["xb"][pair].reshape(256, 768).astype(F32) + mm(o, r["wp"][...])
+        r["x1"][pair] = x1.reshape(2, 128, 768)
+        hat, _ = norm_parts(x1)
+        n2 = (hat * g2 + b2).astype(BF16)
+        r["n2"][pair] = n2.reshape(2, 128, 768)
+        act, slope = gelu_pair(mm(n2, r["w1"][...]))
+        r["act"][pair] = act.astype(BF16).reshape(2, 128, 384)
+        du = (mm_nt(r["dyb"][pair].reshape(256, 768), r["w2"][...]) * slope).astype(BF16)
+        r["du"][pair] = du.reshape(2, 128, 384)
+        r["part"][...] = mm_nt(du, r["w1"][...]).reshape(2, 128, 768)
+        dn.put(j, r["part"][e], r["part"][1 - e])
+
+        @pl.when(j > 0)
+        def _():
+            dn.tx[j - 1] = dn.sum_core(j - 1).astype(BF16)
+            dn.send(j - 1).start()
+
+        return carry
+
+    lax.fori_loop(0, 4, feed, 0)
+
+    grad = mm_tn(r["act"][...].reshape(1024, 384), r["dyb"][...].reshape(1024, 768)).astype(BF16)
+    for k in range(4):
+        ca.own[k, 0] = grad[96 * k : 96 * k + 96, 0:384]
+        ca.own[k, 1] = grad[96 * k : 96 * k + 96, 384:768]
+        ca.prime(k)
+
+    grad = mm_tn(r["n2"][...].reshape(1024, 768), r["du"][...].reshape(1024, 384)).astype(BF16)
+    for i in range(8):
+        r["t1"][i % 2, i // 2] = grad[96 * i : 96 * i + 96]
+    t1_core = remote(r["t1"].at[1 - e], r["t1x"], r["t1_cs"], r["t1_cr"], other)
+    t1_core.start()
+
+    def t1_send(delta, half):
+        src = r["t1"].at[e, chip_at(delta)] if half == 0 else r["t1x"].at[chip_at(delta)]
+        hidden_core = e if half == 0 else 1 - e
+        at = 2 * delta + half
+        return remote(src, ca.own.at[4 + delta, hidden_core], r["t1_s"].at[at], r["t1_r"].at[at], dev(delta))
+
+    def second(j, carry):
+        delta = 3 - j
+        pair = pl.ds(2 * chip_at(delta), 2)
+        r["part"][...] = mm(r["act"][pair].reshape(256, 384), r["w2"][...]).reshape(2, 128, 768)
+        ys.put(j, r["part"][e], r["part"][1 - e])
+        return carry
+
+    lax.fori_loop(0, 4, second, 0)
+    ca.tick(1)
+
+    runs = [r["perm"][4 * e + s] for s in range(4)]
+    n1s = jnp.concatenate([r["n1"][run] for run in runs], axis=0)
+    r["n1s"][...] = n1s
+    r["qo"][...] = mm(n1s, r["wo"][...]).astype(BF16).reshape(2, 256, 576)
+
+    dn2 = dn.result()
+    x1 = r["x1"][b]
+    hat, inv_std = norm_parts(x1)
+    r["lnp"][2:3] = jnp.sum(dn2 * hat, axis=0, keepdims=True)
+    r["lnp"][3:4] = jnp.sum(dn2, axis=0, keepdims=True)
+    dx1 = r["dyb"][b].astype(F32) + norm_back(dn2, hat, inv_std, g2)
+    r["dx1"][...] = dx1
+    low = dx1.astype(BF16)
+    r["dxb"][b] = low
+    do = mm_nt(low, r["wp"][...]).astype(BF16)
+    for i in range(4):
+        r["dos"][i] = do[:, 192 * i : 192 * i + 192]
+    for delta in (3, 2, 1):
+        gdo.to_chip(delta, r["dos"].at[chip_at(delta)]).start()
+    gdo.to_core(r["dos"].at[chip]).start()
+    r["dob"][b] = r["dos"][chip]
+    t1_core.wait_recv()
+    for delta in (3, 2, 1):
+        for half in (0, 1):
+            t1_send(delta, half).start()
+    ca.own[4, e] = r["t1"][e, chip]
+    ca.own[4, 1 - e] = r["t1x"][chip]
+    ca.prime(4)
+    ca.tick(2)
+    gdx.send(r["dxb"].at[b])
+    for delta in (1, 2, 3):
+        gdo.wait_chip(delta)
+    for delta in range(4):
+        gdo.wait_core(delta)
+
+    def attend_back(at, carry):
+        run0, run1 = r["perm"][4 * e + 2 * at], r["perm"][4 * e + 2 * at + 1]
+        do_rows = jnp.concatenate([r["dob"][run0], r["dob"][run1]], axis=0)
+        rows = r["qo"][at]
+        for h in range(3):
+            q = rows[:, 64 * h : 64 * h + 64]
+            k = rows[:, 192 + 64 * h : 192 + 64 * h + 64]
+            v = rows[:, 384 + 64 * h : 384 + 64 * h + 64]
+            g = do_rows[:, 64 * h : 64 * h + 64]
+            s = mm_nt(q, k) * scale
+            p = jnp.exp(s - jnp.max(s, axis=-1, keepdims=True))
+            p = p / jnp.sum(p, axis=-1, keepdims=True)
+            dp = mm_nt(g, v)
+            ds = (p * (dp - jnp.sum(p * dp, axis=-1, keepdims=True))).astype(BF16)
+            r["dq"][at, :, 64 * h : 64 * h + 64] = (mm(ds, k) * scale).astype(BF16)
+            r["dq"][at, :, 192 + 64 * h : 192 + 64 * h + 64] = (mm_tn(ds, q) * scale).astype(BF16)
+            r["dq"][at, :, 384 + 64 * h : 384 + 64 * h + 64] = mm_tn(p.astype(BF16), g).astype(BF16)
+        return carry
+
+    lax.fori_loop(0, 2, attend_back, 0)
+    ca.tick(3)
+
+    dqkv = r["dq"][...].reshape(512, 576)
+    grad = mm_tn(r["n1s"][...], dqkv)
+    for i in range(8):
+        r["tq"][i % 2, i // 2] = grad[96 * i : 96 * i + 96].astype(BF16)
+    tq_core = remote(r["tq"].at[1 - e], r["tqx"], r["tq_cs"], r["tq_cr"], other)
+    tq_core.start()
+
+    dn1_low = mm_nt(dqkv, r["wo"][...]).astype(BF16)
+    r["d1"][pl.ds(4 * e, 4)] = dn1_low.reshape(4, 128, 768)
+    d1_core = remote(r["d1"].at[pl.ds(4 * e, 4)], r["d1"].at[pl.ds(4 * e, 4)], r["d1_cs"], r["d1_cr"], other)
+    d1_core.start()
+
+    def tq_send(delta):
+        return remote(r["tqs"].at[delta], cb.own.at[delta], r["tq_s"].at[delta], r["tq_r"].at[delta], dev(delta))
+
+    def d1_send(delta):
+        return remote(r["d1s"].at[delta], r["d1r"].at[delta], r["d1_s"].at[delta], r["d1_r"].at[delta], dev(delta))
+
+    tq_core.wait_recv()
+    for delta in (3, 2, 1, 0):
+        c = chip_at(delta)
+        total = (r["tq"][e, c].astype(F32) + r["tqx"][c].astype(F32)).astype(BF16)
+        if delta == 0:
+            cb.own[0] = total
+        else:
+            r["tqs"][delta] = total
+            tq_send(delta).start()
+    remote(r["d1"].at[pl.ds(4 - 4 * e, 4)], r["d1"].at[pl.ds(4 - 4 * e, 4)], r["d1_cs"], r["d1_cr"], other).wait_recv()
+    for delta in (3, 2, 1):
+        r["d1s"][delta] = r["d1"][r["inv"][2 * chip_at(delta) + e]]
+        d1_send(delta).start()
+
+    for delta in (1, 2, 3):
+        for half in (0, 1):
+            t1_send(delta, half).wait_recv()
+        ca.prime(4 + delta)
+    ca.tick(4)
+    cb.prime(0)
+    for delta in (1, 2, 3):
+        gdx.wait_chip(delta)
+    ca.tick(5)
+    for delta in range(4):
+        gdx.wait_core(delta)
+    parts = []
+    for i in range(8):
+        o = r["ob"][chip // 2, r["inv"][i]]
+        first = jnp.where(e == 0, o[:, 0:96], o[:, 96:192])
+        second_half = jnp.where(e == 0, o[:, 192:288], o[:, 288:384])
+        parts.append(jnp.where(odd, second_half, first))
+    grad = mm_tn(jnp.concatenate(parts, axis=0), r["dxb"][...].reshape(1024, 768)).astype(BF16)
+    ca.own[8, 0] = grad[:, 0:384]
+    ca.own[8, 1] = grad[:, 384:768]
+    ca.prime(8)
+    ca.tick(6)
+    for j in range(3):
+        ys.tx[j] = ys.sum_core(j).astype(BF16)
+        ys.send(j).start()
+    for delta in (1, 2, 3):
+        tq_send(delta).wait_recv()
+        cb.prime(delta)
+    ca.tick(7)
+    dn1 = r["d1"][r["inv"][b]].astype(F32)
+    for delta in (1, 2, 3):
+        d1_send(delta).wait_recv()
+        dn1 += r["d1r"][delta].astype(F32)
+    hat, inv_std = norm_parts(r["xb"][b].astype(F32))
+    r["lnp"][0:1] = jnp.sum(dn1 * hat, axis=0, keepdims=True)
+    r["lnp"][1:2] = jnp.sum(dn1, axis=0, keepdims=True)
+    r["lnp"][4:8] = jnp.zeros((4, 768), F32)
+    r["o_gin"][...] = (r["dx1"][...] + norm_back(dn1, hat, inv_std, g1)).astype(BF16)
+    ln_core = remote(r["lnp"], r["lnx"].at[0], r["ln_s"].at[0], r["ln_r"].at[0], other)
+    ln_core.start()
+    ca.tick(8)
+    cb.tick(1)
+    ln_core.wait_recv()
+    r["lns"][...] = r["lnp"][...] + r["lnx"][0]
+
+    def ln_send(delta):
+        return remote(r["lns"], r["lnx"].at[delta], r["ln_s"].at[delta], r["ln_r"].at[delta], dev(delta))
+
+    for delta in (3, 2, 1):
+        ln_send(delta).start()
+    ca.tick(9)
+    cb.tick(2)
+    total = r["lns"][...]
+    for delta in (1, 2, 3):
+        ln_send(delta).wait_recv()
+        total += r["lnx"][delta]
+    cc.own[0] = total
+    cc.prime(0)
+    ca.tick(10)
+    cb.tick(3)
+    cc.tick(1)
+    ca.tick(11)
+    cb.tick(4)
+    cc.tick(2)
+    r["o_y"][...] = (r["x1"][b] + ys.result()).astype(BF16)
+    cb.tick(5)
+    cc.tick(3)
+    cb.tick(6)
+
+    gx.finish(r["x"])
+    gdy.finish(r["dy"])
+    gdx.finish(r["dxb"].at[b])
+    gdo.finish(r["dos"].at[chip])
+    for at in range(4):
+        o_core(at).wait_send()
+    dn.finish()
+    ys.finish()
+    t1_core.wait_send()
+    tq_core.wait_send()
+    d1_core.wait_send()
+    for delta in (1, 2, 3):
+        t1_send(delta, 0).wait_send()
+        t1_send(delta, 1).wait_send()
+        tq_send(delta).wait_send()
+        d1_send(delta).wait_send()
+        ln_send(delta).wait_send()
+    ln_core.wait_send()
+    ca.finish()
+    cb.finish()
+    cc.finish()
+
+
+def fast_shards(
+    Z, inputs, crops, ln1_gain, ln1_bias, w_qkv, w_proj, ln2_gain, ln2_bias, w_fc1, w_fc2, cotangent
+):
+    V, D = pltpu.VMEM, pltpu.SemaphoreType.DMA
+    anyspace = pl.BlockSpec(memory_space=pl.ANY)
+    vmem = pl.BlockSpec(memory_space=pltpu.VMEM)
+    smem = pl.BlockSpec(memory_space=pltpu.SMEM)
+    arguments = dict(
+        x=(inputs[0], anyspace),
+        crops=(crops, smem),
+        ln1_gain=(ln1_gain[None], vmem),
+        ln1_bias=(ln1_bias[None], vmem),
+        w_qkv=(w_qkv, anyspace),
+        w_proj=(w_proj, anyspace),
+        ln2_gain=(ln2_gain[None], vmem),
+        ln2_bias=(ln2_bias[None], vmem),
+        w_fc1=(w_fc1, anyspace),
+        w_fc2=(w_fc2, anyspace),
+        dy=(cotangent[0], anyspace),
+    )
+    results = dict(
+        o_y=((128, 768), BF16),
+        o_gin=((128, 768), BF16),
+        o_qkv=((4, 96, 576), BF16),
+        o_proj=((96, 768), BF16),
+        o_fc1=((96, 3072), BF16),
+        o_fc2=((384, 768), BF16),
+        o_ln=((8, 768), F32),
+    )
+    scratch = dict(
+        ld_sem=D((11,)),
+        perm=pltpu.SMEM((8,), jnp.int32),
+        inv=pltpu.SMEM((8,), jnp.int32),
+        xb=V((8, 128, 768), BF16), gx_s=D((8,)), gx_r=D((8,)),
+        dyb=V((8, 128, 768), BF16), gdy_s=D((8,)), gdy_r=D((8,)),
+        dxb=V((8, 128, 768), BF16), gdx_s=D((8,)), gdx_r=D((8,)),
+        dob=V((8, 128, 192), BF16), dos=V((4, 128, 192), BF16), gdo_s=D((8,)), gdo_r=D((8,)),
+        wf=V((768, 1152), BF16), w4=V((3, 768, 256), BF16), wo=V((768, 576), BF16),
+        wp=V((768, 768), BF16), w1=V((768, 384), BF16), w2=V((384, 768), BF16),
+        n1=V((8, 128, 768), BF16), n1s=V((512, 768), BF16), qkv=V((8, 128, 1152), BF16),
+        ob=V((2, 8, 128, 384), BF16), o_s=D((4,)), o_r=D((4,)),
+        x1=V((8, 128, 768), F32), n2=V((8, 128, 768), BF16),
+        act=V((8, 128, 384), BF16), du=V((8, 128, 384), BF16), part=V((2, 128, 768), F32),
+        dx1=V((128, 768), F32),
+        t1=V((2, 4, 96, 384), BF16), t1x=V((4, 96, 384), BF16),
+        t1_cs=D, t1_cr=D, t1_s=D((8,)), t1_r=D((8,)),
+        qo=V((2, 256, 576), BF16), dq=V((2, 256, 576), BF16),
+        tq=V((2, 4, 96, 576), BF16), tqx=V((4, 96, 576), BF16), tqs=V((4, 96, 576), BF16),
+        tq_cs=D, tq_cr=D, tq_s=D((4,)), tq_r=D((4,)),
+        d1=V((8, 128, 768), BF16), d1s=V((4, 128, 768), BF16), d1r=V((4, 128, 768), BF16),
+        d1_cs=D, d1_cr=D, d1_s=D((4,)), d1_r=D((4,)),
+        lnp=V((8, 768), F32), lns=V((8, 768), F32), lnx=V((4, 8, 768), F32), ln_s=D((4,)), ln_r=D((4,)),
+    )
+    for name in ("dn", "ys"):
+        scratch.update(
+            {
+                name + "_ctx": V((4, 128, 768), BF16), name + "_crx": V((4, 128, 768), BF16),
+                name + "_keep": V((4, 128, 768), F32), name + "_tx": V((3, 128, 768), BF16),
+                name + "_rx": V((3, 128, 768), BF16), name + "_cs": D((4,)), name + "_cr": D((4,)),
+                name + "_ss": D((3,)), name + "_sr": D((3,)),
+            }
+        )
+    for name, K, shape, dtype in (
+        ("ca", 9, (2, 96, 384), BF16), ("cb", 4, (96, 576), BF16), ("cc", 1, (8, 768), F32)
+    ):
+        for part in ("own", "rl", "rr", "tu", "td"):
+            scratch[name + "_" + part] = V((K, *shape), dtype)
+        for part in ("su", "sd", "ru", "rd"):
+            scratch[name + "_" + part] = D((K,))
+    names = (*arguments, *results, *scratch)
+    y, gin, gqkv, gproj, gfc1, gfc2, gln = pl.pallas_call(
+        functools.partial(layer_kernel, Z, names),
+        out_shape=[jax.ShapeDtypeStruct(*shape) for shape in results.values()],
+        in_specs=[spec for _, spec in arguments.values()],
+        out_specs=[vmem] * len(results),
+        scratch_shapes=list(scratch.values()),
+        compiler_params=pltpu.CompilerParams(
+            collective_id=0, has_side_effects=True, vmem_limit_bytes=60 * 2**20
+        ),
+    )(*[array for array, _ in arguments.values()])
+    gqkv = gqkv.reshape(4, 96, 3, 192).transpose(1, 2, 0, 3).reshape(96, 2304)
+    mine = lax.dynamic_slice_in_dim(gln, 96 * lax.axis_index("blk"), 96, 1)
+    return (
+        y[None], gin[None], gqkv.astype(F32), gproj.astype(F32), gfc1.astype(F32), gfc2.astype(F32),
+        mine[0], mine[1], mine[2], mine[3],
+    )
+
+
 def solution(mesh):
     placed = (
         P("dp", "blk", None),
@@ -268,8 +951,13 @@
         P(),
         P("dp", "blk", None),
     )
-    return jax.shard_map(
-        shards,
+    def whole(*arrays):
+        one_run = arrays[0].shape[1] == 8 * RUN_ROWS and mesh.shape["blk"] == 8
+        body = functools.partial(fast_shards, mesh.shape["dp"]) if one_run else shards
+        return placed_call(body)(*arrays)
+
+    placed_call = lambda body: jax.shard_map(
+        body,
         mesh=mesh,
         in_specs=placed,
         out_specs=(
@@ -286,3 +974,4 @@
         ),
         check_vma=False,
     )
+    return whole

time: 461 us -> 127 us (0.28)
  waiting for transfers between devices: 307 us -> 0 us
  Pallas kernels: 0 us -> 111 us
  matrix products: 58.8 us -> 0 us
  blocking collectives: 27.4 us -> 0 us
  other arithmetic: 25.2 us -> 2.94 us
  between operations: 15.4 us -> 0.69 us
  local copies, waits for them, and re-layouts: 26.2 us -> 11.6 us
    reduce_scatter x4 -> x0, waiting for transfers between devices: 201 us -> none  [the longest x1 57.6 us: shards(): lax.psum_scatter(grad_fc1.astype(jnp.bfloat16), 'blk', scatter_dimension=...]
    pallas_call x0 -> x1, Pallas kernels: none -> 111 us  [fast_shards(): pl.pallas_call(functools.partial(layer_kernel, Z, names), out_shape=[jax....]
    dot_general x18 -> x0, matrix products: 58.8 us -> none  [the longest x4 16.9 us: contract_rows(): lax.dot_general(left_side, right_side, (((0,), (0,)), ((), ())), preferre...]
    all_gather x2 -> x0, waiting for transfers between devices: 45.4 us -> none  [the longest x1 25.2 us: shards(): lax.all_gather(key_own, 'blk', axis=0, tiled=True)]
    psum x1 -> x0, waiting for transfers between devices: 31.2 us -> none  [shards(): lax.psum(qkv_share.astype(jnp.bfloat16), 'dp').astype(jnp.float32)]
    unnamed x9 -> x0, waiting for transfers between devices: 29.4 us -> none
    unnamed x97 -> x12, local copies, waits for them, and re-layouts: 16.7 us -> 1.45 us
    unnamed x1 -> x0, blocking collectives: 14.5 us -> none
  transfers between devices with their start and end apart: 8 -> 0, of which waited for: 8 -> 0; matrix products, arithmetic and copies ran while one was open for 12% -> 0% of each run, Pallas kernels for 0% -> 0%
where the time goes in v1:
time: 127 us; the launch traced here: 126 us
  Pallas kernels  111 us (87%)
  local copies, waits for them, and re-layouts  11.6 us (9%)
  other arithmetic  2.94 us (2%)
    pallas_call x1, Pallas kernels, fast_shards(): pl.pallas_call(functools.partial(layer_kernel, Z, names), out_shape=[jax....  111 us
    convert_element_type x3, local copies, waits for them, and re-layouts, fast_shards(): gqkv.astype(F32)  3.77 us

profile of v1, /device:TPU:0, one launch (start us, length us, event | category | flops | bytes accessed | tf_op | source)
XLA Modules:
  0.0 126.3 jit_solution(6330004061407459670)
XLA Ops:
  0.6 1.3 %broadcast_in_dim.18.refs_2_ = f32[1,768]{1,0:T(1,128)} reshape(f32[768]{0:T(1024)} %param.13) | data formatting | bytes 6144 | tf_op jit(solution)/shard_map/broadcast_in_dim | solution.py:862
  1.9 1.3 %broadcast_in_dim.19.refs_3_ = f32[1,768]{1,0:T(1,128)} reshape(f32[768]{0:T(1024)} %param.14) | data formatting | bytes 6144 | tf_op jit(solution)/shard_map/broadcast_in_dim | solution.py:863
  3.2 1.3 %broadcast_in_dim.20.refs_6_ = f32[1,768]{1,0:T(1,128)} reshape(f32[768]{0:T(1024)} %param.17) | data formatting | bytes 6144 | tf_op jit(solution)/shard_map/broadcast_in_dim | solution.py:866
  4.4 1.3 %broadcast_in_dim.21.refs_7_ = f32[1,768]{1,0:T(1,128)} reshape(f32[768]{0:T(1024)} %param.18) | data formatting | bytes 6144 | tf_op jit(solution)/shard_map/broadcast_in_dim | solution.py:867
  5.7 111.1 %shard_map.186 = (bf16[128,768]{1,0:T(8,128)(2,1)}, bf16[128,768]{1,0:T(8,128)(2,1)}, bf16[4,96,576]{2,1,0:T(8,128)(2,1)}, bf16[96,768]{1,0:T(8,128)(2,1)}, bf16...) custom-call(bf16[128,768]{1,0:T(8,128)(2,1)} %bitcast.16, s32[1,1024]{1,0:T(1,128)} %refs_1_.1, ...), custom_call_target="tpu_custom_call" | custom-call | tf_op jit(solution)/shard_map/pallas_call | solution.py:922
  116.8 0.8 constant_dynamic-slice_fusion
  117.6 0.5 slice_bitcast_fusion
  118.1 1.3 copy.23
  119.4 0.8 copy.24
  120.3 0.0 copy-start.1
  120.3 1.7 %reshape.26 = f32[96,2304]{1,0:T(8,128)} reshape(f32[96,3,4,192]{3,2,1,0:T(4,128)S(1)} %copy.24) | data formatting | bytes 1769472 | tf_op jit(solution)/shard_map/convert_element_type | solution.py:935
  121.9 0.0 copy-start
  121.9 0.0 copy-done.1
  121.9 1.1 convert_element_type.26
  123.1 0.0 copy-start.4
  123.1 0.0 copy-start.3
  123.1 0.1 copy-done
  123.1 0.0 copy-start.2
  123.1 1.1 convert_element_type.27
  124.2 0.0 copy-done.4
  124.2 0.7 convert_element_type.25
  125.0 0.0 copy-done.3
  125.0 0.7 copy.27
  125.7 0.0 copy-done.2
  125.7 0.7 copy.28
Async XLA Ops:
  120.3 1.7 %copy-start.1 = (bf16[96,3072]{1,0:T(8,128)(2,1)S(1)}, bf16[96,3072]{1,0:T(8,128)(2,1)}, u32[]{:S(2)}) copy-start(bf16[96,3072]{1,0:T(8,128)(2,1)} %get-tuple-element.21) | copy-start | bytes 1769476
  121.9 1.2 copy-start
  123.1 1.2 copy-start.4
  123.1 1.9 %copy-start.3 = (bf16[128,768]{1,0:T(8,128)(2,1)S(1)}, bf16[128,768]{1,0:T(8,128)(2,1)}, u32[]{:S(2)}) copy-start(bf16[128,768]{1,0:T(8,128)(2,1)} %get-tuple-element.17) | copy-start | bytes 589828
  123.1 2.5 %copy-start.2 = (bf16[128,768]{1,0:T(8,128)(2,1)S(1)}, bf16[128,768]{1,0:T(8,128)(2,1)}, u32[]{:S(2)}) copy-start(bf16[128,768]{1,0:T(8,128)(2,1)} %get-tuple-element.18) | copy-start | bytes 589828

commit v2 on v1

--- a/solution.py
+++ b/solution.py
@@ -317,32 +317,26 @@
         return (z, 2 * chip_at(delta) + e)
 
     other = (z, b + 1 - 2 * e)
-    slot_other = b + 1 - 2 * e
 
     def remote(src, dst, send_sem, recv_sem, device):
+        sems = [s[0].at[s[1]] if isinstance(s, tuple) else s for s in (send_sem, recv_sem)]
         return pltpu.make_async_remote_copy(
-            src_ref=src, dst_ref=dst, send_sem=send_sem, recv_sem=recv_sem,
+            src_ref=src, dst_ref=dst, send_sem=sems[0], recv_sem=sems[1],
             device_id=device, device_id_type=MESH,
         )
 
-    loads = []
-
-    def load(src, dst, at):
-        copy = pltpu.make_async_copy(src, dst, r["ld_sem"].at[at])
-        copy.start()
-        loads.append(copy)
-
-    load(r["x"], r["xb"].at[b], 0)
-    for t in range(3):
-        first = pl.multiple_of(768 * t + 384 * e, 128)
-        load(r["w_qkv"].at[:, pl.ds(first, 384)], r["wf"].at[:, pl.ds(384 * t, 384)], 1 + t)
-    load(r["w_proj"], r["wp"], 4)
-    load(r["w_fc1"].at[:, pl.ds(pl.multiple_of(384 * b, 128), 384)], r["w1"], 5)
-    load(r["w_fc2"].at[pl.ds(pl.multiple_of(384 * b, 128), 384)], r["w2"], 6)
-    load(r["dy"], r["dyb"].at[b], 7)
-    for t in range(3):
-        first = pl.multiple_of(768 * t + 192 * chip - 64 * lax.rem(chip, 2), 128)
-        load(r["w_qkv"].at[:, pl.ds(first, 256)], r["w4"].at[t], 8 + t)
+    loads = {}
+
+    def load(name, src, dst):
+        loads[name] = pltpu.make_async_copy(src, dst, r["ld_sem"].at[len(loads)])
+        loads[name].start()
+
+    load("x", r["x"], r["xb"].at[b])
+    load("w_qkv", r["w_qkv"], r["wq"])
+    load("w_proj", r["w_proj"], r["wp"])
+    load("dy", r["dy"], r["dyb"].at[b])
+    load("w_fc1", r["w_fc1"], r["w1"])
+    load("w_fc2", r["w_fc2"], r["w2"])
 
     bar = pltpu.get_barrier_semaphore()
     for target in (other, dev(1), dev(2), dev(3)):
@@ -362,46 +356,56 @@
         def __init__(self, buf, ss, rs):
             self.buf, self.ss, self.rs = buf, ss, rs
 
-        def to_chip(self, delta, src):
-            return remote(src, self.buf.at[b], self.ss.at[2 * delta], self.rs.at[2 * delta], dev(delta))
-
-        def to_core(self, src):
-            return remote(src, self.buf.at[b], self.ss.at[1], self.rs.at[1], other)
-
         def slot(self, m):
             return 2 * chip_at(m // 2) + (e if m % 2 == 0 else 1 - e)
 
+        def hop(self, delta, src=None):
+            at = b if src is not None else self.slot(2 * delta)
+            src = self.buf.at[at] if src is None else src
+            return remote(src, self.buf.at[at], (self.ss, 2 * delta), (self.rs, 2 * delta), dev(delta))
+
+        def half(self, part, delta, towards):
+            at = (self.slot(2 * delta), pl.ds(64 * part, 64))
+            return remote(self.buf.at[at], self.buf.at[at], (self.ss, 6 + 2 * part), (self.rs, 6 + 2 * part), dev(towards))
+
+        def core(self, delta, src=None):
+            at = b if src is not None else self.slot(2 * delta)
+            src = self.buf.at[at] if src is None else src
+            return remote(src, self.buf.at[at], (self.ss, 2 * delta + 1), (self.rs, 2 * delta + 1), other)
+
         def send(self, src):
-            for delta in (3, 2, 1):
-                self.to_chip(delta, src).start()
-            self.to_core(src).start()
-
-        def forward(self, delta):
-            at = self.slot(2 * delta)
-            return remote(
-                self.buf.at[at], self.buf.at[at], self.ss.at[2 * delta + 1],
-                self.rs.at[2 * delta + 1], other,
-            )
-
-        def wait_chip(self, delta):
-            at = self.slot(2 * delta)
-            remote(self.buf.at[at], self.buf.at[at], self.ss.at[2 * delta], self.rs.at[2 * delta], dev(delta)).wait_recv()
-            self.forward(delta).start()
+            self.hop(1, src).start()
+            self.hop(2, src).start()
+            self.core(0, src).start()
+
+        def pass_on(self):
+            self.hop(1).wait_recv()
+            self.half(0, 1, 2).start()
+            self.hop(2).wait_recv()
+            self.half(1, 2, 1).start()
+            self.core(1).start()
+            self.core(2).start()
+
+        def pass_diagonal(self):
+            self.half(0, 3, 2).wait_recv()
+            self.half(1, 3, 1).wait_recv()
+            self.core(3).start()
 
         def wait_core(self, delta):
             at = self.slot(2 * delta + 1)
-            remote(self.buf.at[at], self.buf.at[at], self.ss.at[2 * delta + 1], self.rs.at[2 * delta + 1], other).wait_recv()
+            remote(self.buf.at[at], self.buf.at[at], (self.ss, 2 * delta + 1), (self.rs, 2 * delta + 1), other).wait_recv()
 
         def finish(self, src):
+            self.hop(1, src).wait_send()
+            self.hop(2, src).wait_send()
+            self.half(0, 1, 2).wait_send()
+            self.half(1, 2, 1).wait_send()
+            self.core(0, src).wait_send()
             for delta in (1, 2, 3):
-                self.to_chip(delta, src).wait_send()
-                self.forward(delta).wait_send()
-            self.to_core(src).wait_send()
+                self.core(delta).wait_send()
 
     gx = Gather(r["xb"], r["gx_s"], r["gx_r"])
     gdy = Gather(r["dyb"], r["gdy_s"], r["gdy_r"])
-    gdx = Gather(r["dxb"], r["gdx_s"], r["gdx_r"])
-    gdo = Gather(r["dob"], r["gdo_s"], r["gdo_r"])
 
     class Chain:
         def __init__(self, name, K, dtype, sink):
@@ -410,10 +414,10 @@
                 setattr(self, part, r[name + "_" + part])
 
         def up(self, src, k):
-            return remote(src, self.rl.at[k], self.su.at[k], self.ru.at[k], (z + 1, b))
+            return remote(src, self.rl.at[k], (self.su, k), (self.ru, k), (z + 1, b))
 
         def down(self, src, k):
-            return remote(src, self.rr.at[k], self.sd.at[k], self.rd.at[k], (z - 1, b))
+            return remote(src, self.rr.at[k], (self.sd, k), (self.rd, k), (z - 1, b))
 
         def prime(self, k):
             if Z == 1:
@@ -496,48 +500,13 @@
         r["o_qkv"][chip_at(k)] = total.astype(BF16)
 
     def sink_c(k, total):
-        r["o_ln"][...] = total
+        for i in range(8):
+            r["lnc"][i] = total[:, 96 * i : 96 * i + 96]
+        r["o_ln"][...] = r["lnc"][b]
 
     ca = Chain("ca", 9, BF16, sink_a)
     cb = Chain("cb", 4, BF16, sink_b)
     cc = Chain("cc", 1, F32, sink_c)
-
-    class Scatter:
-        def __init__(self, name):
-            for part in ("ctx", "crx", "keep", "tx", "rx", "cs", "cr", "ss", "sr"):
-                setattr(self, part, r[name + "_" + part])
-
-        def core(self, j):
-            return remote(self.ctx.at[j], self.crx.at[j], self.cs.at[j], self.cr.at[j], other)
-
-        def send(self, j):
-            delta = 3 - j
-            return remote(self.tx.at[j], self.rx.at[j], self.ss.at[j], self.sr.at[j], dev(delta))
-
-        def put(self, j, mine, theirs):
-            self.keep[j] = mine
-            self.ctx[j] = theirs.astype(BF16)
-            self.core(j).start()
-
-        def sum_core(self, j):
-            self.core(j).wait_recv()
-            return self.keep[j] + self.crx[j].astype(F32)
-
-        def result(self):
-            total = self.sum_core(3)
-            for j in range(3):
-                self.send(j).wait_recv()
-                total += self.rx[j].astype(F32)
-            return total
-
-        def finish(self):
-            for j in range(4):
-                self.core(j).wait_send()
-            for j in range(3):
-                self.send(j).wait_send()
-
-    dn = Scatter("dn")
-    ys = Scatter("ys")
 
     gx.send(r["x"])
 
@@ -555,68 +524,82 @@
             run = run + jnp.where(places[i] == s, i, 0)
         r["perm"][s] = run
 
-    for copy in loads[:4]:
-        copy.wait()
-    for copy in loads[8:]:
-        copy.wait()
-    odd = lax.rem(chip, 2) == 1
-    for t in range(3):
-        r["wo"][:, 192 * t : 192 * t + 192] = jnp.where(odd, r["w4"][t, :, 64:256], r["w4"][t, :, 0:192])
-
-    g1, b1 = r["ln1_gain"][...], r["ln1_bias"][...]
-    g2, b2 = r["ln2_gain"][...], r["ln2_bias"][...]
-
-    for delta in range(4):
-        if delta > 0:
-            gx.wait_chip(delta)
-            gdy.to_chip(delta, r["dy"]).start()
-        else:
-            gdy.to_core(r["dy"]).start()
+    g1, b1 = r["ln1_gain"][...].reshape(1, 768), r["ln1_bias"][...].reshape(1, 768)
+    g2, b2 = r["ln2_gain"][...].reshape(1, 768), r["ln2_bias"][...].reshape(1, 768)
+
+    loads["x"].wait()
+    loads["w_qkv"].wait()
+    for i in range(4):
+        for t in range(3):
+            first = 768 * t + 192 * i
+            r["wo"][i, :, 128 * t : 128 * t + 128] = r["wq"][:, first : first + 128]
+            r["wo"][i, :, 384 + 64 * t : 448 + 64 * t] = r["wq"][:, first + 128 : first + 192]
+
+    def project(delta):
         gx.wait_core(delta)
         pair = pl.ds(2 * chip_at(delta), 2)
         hat, _ = norm_parts(r["xb"][pair].reshape(256, 768).astype(F32))
         normed = (hat * g1 + b1).astype(BF16)
         r["n1"][pair] = normed.reshape(2, 128, 768)
-        r["qkv"][pair] = mm(normed, r["wf"][...]).astype(BF16).reshape(2, 128, 1152)
+        for t in range(3):
+            out = mm(normed, r["wq"][:, pl.ds(pl.multiple_of(768 * t + 384 * e, 128), 384)])
+            out = out * scale if t == 0 else out
+            r["qkv"][pair, :, 384 * t : 384 * t + 384] = out.astype(BF16).reshape(2, 128, 384)
+
+    project(0)
+    gx.pass_on()
+    gdy.send(r["dy"])
+    project(1)
+    project(2)
+    gx.pass_diagonal()
+    project(3)
+
+    low_lanes = lax.broadcasted_iota(jnp.int32, (1, 128), 1) < HEAD
+
+    def stack(two):
+        none = jnp.zeros_like(two)
+        return jnp.concatenate([jnp.where(low_lanes, two, none), jnp.where(low_lanes, none, two)], axis=0)
 
     def o_core(at):
-        return remote(r["ob"].at[e, pl.ds(2 * at, 2)], r["ob"].at[e, pl.ds(2 * at, 2)], r["o_s"].at[at], r["o_r"].at[at], other)
+        place = (e, pl.ds(2 * at, 2))
+        return remote(r["ob"].at[place], r["ob"].at[place], (r["o_s"], at), (r["o_r"], at), other)
 
     def attend(at, carry):
         run0, run1 = r["perm"][2 * at], r["perm"][2 * at + 1]
-        rows = jnp.concatenate([r["qkv"][run0], r["qkv"][run1]], axis=0)
         outs = []
-        for h in range(6):
-            q = rows[:, 64 * h : 64 * h + 64]
-            k = rows[:, 384 + 64 * h : 384 + 64 * h + 64]
-            v = rows[:, 768 + 64 * h : 768 + 64 * h + 64]
-            s = mm_nt(q, k) * scale
+        for h in range(3):
+            q, k, v = [
+                jnp.concatenate(
+                    [r["qkv"][run, :, 384 * t + 128 * h : 384 * t + 128 * h + 128] for run in (run0, run1)],
+                    axis=0,
+                )
+                for t in range(3)
+            ]
+            s = mm_nt(stack(q), k)
             p = jnp.exp(s - jnp.max(s, axis=-1, keepdims=True))
-            p = (p / jnp.sum(p, axis=-1, keepdims=True)).astype(BF16)
-            outs.append(mm(p, v))
+            o = mm(p.astype(BF16), v) / jnp.sum(p, axis=-1, keepdims=True)
+            outs.append(jnp.where(low_lanes, o[0:256], o[256:512]))
         low = jnp.concatenate(outs, axis=1).astype(BF16)
         r["ob"][e, pl.ds(2 * at, 2)] = low.reshape(2, 128, 384)
         o_core(at).start()
         return carry
 
-    lax.fori_loop(0, 4, attend, 0)
-
-    for delta in (1, 2, 3):
-        gdy.wait_chip(delta)
-    for delta in range(4):
-        gdy.wait_core(delta)
-    for copy in loads[4:8]:
-        copy.wait()
+    lax.fori_loop(0, 3, attend, 0)
+    gdy.pass_on()
+    attend(3, 0)
+    for name in ("w_proj", "w_fc1", "w_fc2", "dy"):
+        loads[name].wait()
     for at in range(4):
-        remote(r["ob"].at[1 - e, pl.ds(2 * at, 2)], r["ob"].at[1 - e, pl.ds(2 * at, 2)], r["o_s"].at[at], r["o_r"].at[at], other).wait_recv()
+        place = (1 - e, pl.ds(2 * at, 2))
+        remote(r["ob"].at[place], r["ob"].at[place], (r["o_s"], at), (r["o_r"], at), other).wait_recv()
 
     def o_rows(run):
         at = r["inv"][run]
         return jnp.concatenate([r["ob"][0, at], r["ob"][1, at]], axis=1)
 
-    def feed(j, carry):
-        delta = 3 - j
-        c = chip_at(delta)
+    own_hidden = pl.ds(pl.multiple_of(384 * b, 128), 384)
+
+    def feed(c, carry):
         pair = pl.ds(2 * c, 2)
         o = jnp.concatenate([o_rows(2 * c), o_rows(2 * c + 1)], axis=0)
         x1 = r["xb"][pair].reshape(256, 768).astype(F32) + mm(o, r["wp"][...])
@@ -624,21 +607,15 @@
         hat, _ = norm_parts(x1)
         n2 = (hat * g2 + b2).astype(BF16)
         r["n2"][pair] = n2.reshape(2, 128, 768)
-        act, slope = gelu_pair(mm(n2, r["w1"][...]))
+        act, slope = gelu_pair(mm(n2, r["w1"][:, own_hidden]))
         r["act"][pair] = act.astype(BF16).reshape(2, 128, 384)
-        du = (mm_nt(r["dyb"][pair].reshape(256, 768), r["w2"][...]) * slope).astype(BF16)
-        r["du"][pair] = du.reshape(2, 128, 384)
-        r["part"][...] = mm_nt(du, r["w1"][...]).reshape(2, 128, 768)
-        dn.put(j, r["part"][e], r["part"][1 - e])
-
-        @pl.when(j > 0)
-        def _():
-            dn.tx[j - 1] = dn.sum_core(j - 1).astype(BF16)
-            dn.send(j - 1).start()
-
+        r["slope"][pair] = slope.reshape(2, 128, 384)
         return carry
 
     lax.fori_loop(0, 4, feed, 0)
+    gdy.pass_diagonal()
+    for delta in range(4):
+        gdy.wait_core(delta)
 
     grad = mm_tn(r["act"][...].reshape(1024, 384), r["dyb"][...].reshape(1024, 768)).astype(BF16)
     for k in range(4):
@@ -646,6 +623,56 @@
         ca.own[k, 1] = grad[96 * k : 96 * k + 96, 384:768]
         ca.prime(k)
 
+    n2_own = r["n2"][b]
+    dy_own = r["dyb"][b]
+    r["y"][...] = r["x1"][b]
+    r["dn2"][...] = jnp.zeros((128, 768), F32)
+
+    def own_rows(i, carry):
+        part = pl.ds(pl.multiple_of(768 * i, 128), 768)
+        act, slope = gelu_pair(mm(r["n2"][b], r["w1"][:, part]))
+        du = (mm_nt(r["dyb"][b], r["w2"][part]) * slope).astype(BF16)
+        r["dn2"][...] += mm_nt(du, r["w1"][:, part])
+        r["y"][...] += mm(act.astype(BF16), r["w2"][part])
+        return carry
+
+    lax.fori_loop(0, 4, own_rows, 0)
+    r["o_y"][...] = r["y"][...].astype(BF16)
+
+    dn2 = r["dn2"][...]
+    hat, inv_std = norm_parts(r["x1"][b])
+    r["lnp"][2:3] = jnp.sum(dn2 * hat, axis=0, keepdims=True)
+    r["lnp"][3:4] = jnp.sum(dn2, axis=0, keepdims=True)
+    dx1 = dy_own.astype(F32) + norm_back(dn2, hat, inv_std, g2)
+    r["dx1"][...] = dx1
+    low = dx1.astype(BF16)
+    do = mm_nt(low, r["wp"][...]).astype(BF16)
+    for i in range(4):
+        r["dos"][i] = do[:, 192 * i : 192 * i + 192]
+
+    def do_send(delta):
+        return remote(r["dos"].at[chip_at(delta)], r["dob"].at[b], (r["do_s"], 2 * delta), (r["do_r"], 2 * delta), dev(delta))
+
+    def do_slot(m):
+        return 2 * chip_at(m // 2) + (e if m % 2 == 0 else 1 - e)
+
+    def do_core(delta):
+        src = r["dos"].at[chip] if delta == 0 else r["dob"].at[do_slot(2 * delta)]
+        return remote(src, r["dob"].at[do_slot(2 * delta)], (r["do_s"], 2 * delta + 1), (r["do_r"], 2 * delta + 1), other)
+
+    for delta in (3, 2, 1):
+        do_send(delta).start()
+    do_core(0).start()
+    r["dob"][b] = r["dos"][chip]
+    ca.tick(1)
+
+    def back_hidden(c, carry):
+        pair = pl.ds(2 * c, 2)
+        da = mm_nt(r["dyb"][pair].reshape(256, 768), r["w2"][own_hidden])
+        r["du"][pair] = (da * r["slope"][pair].reshape(256, 384)).astype(BF16).reshape(2, 128, 384)
+        return carry
+
+    lax.fori_loop(0, 4, back_hidden, 0)
     grad = mm_tn(r["n2"][...].reshape(1024, 768), r["du"][...].reshape(1024, 384)).astype(BF16)
     for i in range(8):
         r["t1"][i % 2, i // 2] = grad[96 * i : 96 * i + 96]
@@ -656,93 +683,82 @@
         src = r["t1"].at[e, chip_at(delta)] if half == 0 else r["t1x"].at[chip_at(delta)]
         hidden_core = e if half == 0 else 1 - e
         at = 2 * delta + half
-        return remote(src, ca.own.at[4 + delta, hidden_core], r["t1_s"].at[at], r["t1_r"].at[at], dev(delta))
-
-    def second(j, carry):
-        delta = 3 - j
-        pair = pl.ds(2 * chip_at(delta), 2)
-        r["part"][...] = mm(r["act"][pair].reshape(256, 384), r["w2"][...]).reshape(2, 128, 768)
-        ys.put(j, r["part"][e], r["part"][1 - e])
-        return carry
-
-    lax.fori_loop(0, 4, second, 0)
-    ca.tick(1)
-
-    runs = [r["perm"][4 * e + s] for s in range(4)]
-    n1s = jnp.concatenate([r["n1"][run] for run in runs], axis=0)
-    r["n1s"][...] = n1s
-    r["qo"][...] = mm(n1s, r["wo"][...]).astype(BF16).reshape(2, 256, 576)
-
-    dn2 = dn.result()
-    x1 = r["x1"][b]
-    hat, inv_std = norm_parts(x1)
-    r["lnp"][2:3] = jnp.sum(dn2 * hat, axis=0, keepdims=True)
-    r["lnp"][3:4] = jnp.sum(dn2, axis=0, keepdims=True)
-    dx1 = r["dyb"][b].astype(F32) + norm_back(dn2, hat, inv_std, g2)
-    r["dx1"][...] = dx1
-    low = dx1.astype(BF16)
-    r["dxb"][b] = low
-    do = mm_nt(low, r["wp"][...]).astype(BF16)
-    for i in range(4):
-        r["dos"][i] = do[:, 192 * i : 192 * i + 192]
-    for delta in (3, 2, 1):
-        gdo.to_chip(delta, r["dos"].at[chip_at(delta)]).start()
-    gdo.to_core(r["dos"].at[chip]).start()
-    r["dob"][b] = r["dos"][chip]
+        return remote(src, ca.own.at[4 + delta, hidden_core], (r["t1_s"], at), (r["t1_r"], at), dev(delta))
+
+    grad = mm_tn(o_rows(b), low).astype(BF16)
+    for i in range(8):
+        r["tp"][i % 2, i // 2] = grad[96 * i : 96 * i + 96]
+    tp_core = remote(r["tp"].at[1 - e], r["tpx"], r["tp_cs"], r["tp_cr"], other)
+    tp_core.start()
+
+    def tp_send(delta):
+        return remote(r["tps"].at[delta], r["tpr"].at[delta], (r["tp_s"], delta), (r["tp_r"], delta), dev(delta))
+
+    for s in range(4):
+        r["n1s"][s] = r["n1"][r["perm"][4 * e + s]]
+    r["qo"][...] = mm(r["n1s"][...].reshape(512, 768), r["wo"][chip]).astype(BF16).reshape(2, 256, 576)
+    ca.tick(2)
+
+    for delta in (1, 2, 3):
+        do_send(delta).wait_recv()
+        do_core(delta).start()
     t1_core.wait_recv()
-    for delta in (3, 2, 1):
+    for delta in (1, 2, 3):
         for half in (0, 1):
             t1_send(delta, half).start()
     ca.own[4, e] = r["t1"][e, chip]
     ca.own[4, 1 - e] = r["t1x"][chip]
     ca.prime(4)
-    ca.tick(2)
-    gdx.send(r["dxb"].at[b])
-    for delta in (1, 2, 3):
-        gdo.wait_chip(delta)
     for delta in range(4):
-        gdo.wait_core(delta)
-
-    def attend_back(at, carry):
-        run0, run1 = r["perm"][4 * e + 2 * at], r["perm"][4 * e + 2 * at + 1]
-        do_rows = jnp.concatenate([r["dob"][run0], r["dob"][run1]], axis=0)
-        rows = r["qo"][at]
-        for h in range(3):
-            q = rows[:, 64 * h : 64 * h + 64]
-            k = rows[:, 192 + 64 * h : 192 + 64 * h + 64]
-            v = rows[:, 384 + 64 * h : 384 + 64 * h + 64]
-            g = do_rows[:, 64 * h : 64 * h + 64]
-            s = mm_nt(q, k) * scale
-            p = jnp.exp(s - jnp.max(s, axis=-1, keepdims=True))
-            p = p / jnp.sum(p, axis=-1, keepdims=True)
-            dp = mm_nt(g, v)
-            ds = (p * (dp - jnp.sum(p * dp, axis=-1, keepdims=True))).astype(BF16)
-            r["dq"][at, :, 64 * h : 64 * h + 64] = (mm(ds, k) * scale).astype(BF16)
-            r["dq"][at, :, 192 + 64 * h : 192 + 64 * h + 64] = (mm_tn(ds, q) * scale).astype(BF16)
-            r["dq"][at, :, 384 + 64 * h : 384 + 64 * h + 64] = mm_tn(p.astype(BF16), g).astype(BF16)
-        return carry
-
-    lax.fori_loop(0, 2, attend_back, 0)
+        at = do_slot(2 * delta + 1)
+        remote(r["dob"].at[at], r["dob"].at[at], (r["do_s"], 2 * delta + 1), (r["do_r"], 2 * delta + 1), other).wait_recv()
+
+    def attend_back(at, heads):
+        runs = [r["perm"][4 * e + 2 * at + i] for i in range(2)]
+        if heads == 2:
+            g = jnp.concatenate([r["dob"][run, :, 0:128] for run in runs], axis=0)
+            q, k, v = [r["qo"][at, :, 128 * t : 128 * t + 128] for t in range(3)]
+            q, g = stack(q), stack(g)
+        else:
+            g = jnp.concatenate([r["dob"][run, :, 128:192] for run in runs], axis=0)
+            q, k, v = [r["qo"][at, :, 384 + 64 * t : 448 + 64 * t] for t in range(3)]
+        q = (q.astype(F32) * scale).astype(BF16)
+        s = mm_nt(q, k)
+        p = jnp.exp(s - jnp.max(s, axis=-1, keepdims=True))
+        p = p / jnp.sum(p, axis=-1, keepdims=True)
+        dp = mm_nt(g, v)
+        ds = (p * (dp - jnp.sum(p * dp, axis=-1, keepdims=True))).astype(BF16)
+        dq = mm(ds, k) * scale
+        dk = mm_tn(ds, q)
+        dv = mm_tn(p.astype(BF16), g)
+        mine = pl.ds(2 * (2 * e + at), 2)
+        if heads == 2:
+            dq = jnp.where(low_lanes, dq[0:256], dq[256:512])
+        first, wide = (0, 128) if heads == 2 else (384, 64)
+        for t, part in enumerate((dq, dk, dv)):
+            r["dq"][mine, :, first + wide * t : first + wide * t + wide] = part.astype(BF16).reshape(2, 128, wide)
+
+    attend_back(0, 2)
+    attend_back(0, 1)
     ca.tick(3)
-
-    dqkv = r["dq"][...].reshape(512, 576)
-    grad = mm_tn(r["n1s"][...], dqkv)
+    attend_back(1, 2)
+    attend_back(1, 1)
+
+    dq_core = remote(r["dq"].at[pl.ds(4 * e, 4)], r["dq"].at[pl.ds(4 * e, 4)], r["dq_cs"], r["dq_cr"], other)
+    dq_core.start()
+    grad = mm_tn(r["n1s"][...].reshape(512, 768), r["dq"][pl.ds(4 * e, 4)].reshape(512, 576))
     for i in range(8):
         r["tq"][i % 2, i // 2] = grad[96 * i : 96 * i + 96].astype(BF16)
     tq_core = remote(r["tq"].at[1 - e], r["tqx"], r["tq_cs"], r["tq_cr"], other)
     tq_core.start()
 
-    dn1_low = mm_nt(dqkv, r["wo"][...]).astype(BF16)
-    r["d1"][pl.ds(4 * e, 4)] = dn1_low.reshape(4, 128, 768)
-    d1_core = remote(r["d1"].at[pl.ds(4 * e, 4)], r["d1"].at[pl.ds(4 * e, 4)], r["d1_cs"], r["d1_cr"], other)
-    d1_core.start()
-
     def tq_send(delta):
-        return remote(r["tqs"].at[delta], cb.own.at[delta], r["tq_s"].at[delta], r["tq_r"].at[delta], dev(delta))
-
-    def d1_send(delta):
-        return remote(r["d1s"].at[delta], r["d1r"].at[delta], r["d1_s"].at[delta], r["d1_r"].at[delta], dev(delta))
-
+        return remote(r["tqs"].at[delta], cb.own.at[delta], (r["tq_s"], delta), (r["tq_r"], delta), dev(delta))
+
+    def dq_send(delta):
+        return remote(r["dqs"].at[delta], r["dqr"].at[delta], (r["dq_s"], delta), (r["dq_r"], delta), dev(delta))
+
+    ca.tick(4)
     tq_core.wait_recv()
     for delta in (3, 2, 1, 0):
         c = chip_at(delta)
@@ -752,101 +768,109 @@
         else:
             r["tqs"][delta] = total
             tq_send(delta).start()
-    remote(r["d1"].at[pl.ds(4 - 4 * e, 4)], r["d1"].at[pl.ds(4 - 4 * e, 4)], r["d1_cs"], r["d1_cr"], other).wait_recv()
+    at = pl.ds(4 - 4 * e, 4)
+    remote(r["dq"].at[at], r["dq"].at[at], r["dq_cs"], r["dq_cr"], other).wait_recv()
     for delta in (3, 2, 1):
-        r["d1s"][delta] = r["d1"][r["inv"][2 * chip_at(delta) + e]]
-        d1_send(delta).start()
+        r["dqs"][delta] = r["dq"][r["inv"][2 * chip_at(delta) + e]]
+        dq_send(delta).start()
+    tp_core.wait_recv()
+    for delta in (3, 2, 1, 0):
+        c = chip_at(delta)
+        r["tps"][delta] = (r["tp"][e, c].astype(F32) + r["tpx"][c].astype(F32)).astype(BF16)
+        if delta > 0:
+            tp_send(delta).start()
 
     for delta in (1, 2, 3):
         for half in (0, 1):
             t1_send(delta, half).wait_recv()
         ca.prime(4 + delta)
-    ca.tick(4)
+    ca.tick(5)
     cb.prime(0)
-    for delta in (1, 2, 3):
-        gdx.wait_chip(delta)
-    ca.tick(5)
-    for delta in range(4):
-        gdx.wait_core(delta)
-    parts = []
-    for i in range(8):
-        o = r["ob"][chip // 2, r["inv"][i]]
-        first = jnp.where(e == 0, o[:, 0:96], o[:, 96:192])
-        second_half = jnp.where(e == 0, o[:, 192:288], o[:, 288:384])
-        parts.append(jnp.where(odd, second_half, first))
-    grad = mm_tn(jnp.concatenate(parts, axis=0), r["dxb"][...].reshape(1024, 768)).astype(BF16)
-    ca.own[8, 0] = grad[:, 0:384]
-    ca.own[8, 1] = grad[:, 384:768]
-    ca.prime(8)
-    ca.tick(6)
-    for j in range(3):
-        ys.tx[j] = ys.sum_core(j).astype(BF16)
-        ys.send(j).start()
     for delta in (1, 2, 3):
         tq_send(delta).wait_recv()
         cb.prime(delta)
-    ca.tick(7)
-    dn1 = r["d1"][r["inv"][b]].astype(F32)
+    ca.tick(6)
+    dn1 = mm_nt(r["dq"][r["inv"][b]], r["wo"][chip])
     for delta in (1, 2, 3):
-        d1_send(delta).wait_recv()
-        dn1 += r["d1r"][delta].astype(F32)
+        dq_send(delta).wait_recv()
+        dn1 += mm_nt(r["dqr"][delta], r["wo"][chip_at(delta)])
     hat, inv_std = norm_parts(r["xb"][b].astype(F32))
     r["lnp"][0:1] = jnp.sum(dn1 * hat, axis=0, keepdims=True)
     r["lnp"][1:2] = jnp.sum(dn1, axis=0, keepdims=True)
     r["lnp"][4:8] = jnp.zeros((4, 768), F32)
     r["o_gin"][...] = (r["dx1"][...] + norm_back(dn1, hat, inv_std, g1)).astype(BF16)
-    ln_core = remote(r["lnp"], r["lnx"].at[0], r["ln_s"].at[0], r["ln_r"].at[0], other)
+    ln_core = remote(r["lnp"], r["lnx"].at[0], (r["ln_s"], 0), (r["ln_r"], 0), other)
     ln_core.start()
+    total = r["tps"][0].astype(F32)
+    for delta in (1, 2, 3):
+        tp_send(delta).wait_recv()
+        total += r["tpr"][delta].astype(F32)
+    ca.own[8, 0] = total[:, 0:384].astype(BF16)
+    ca.own[8, 1] = total[:, 384:768].astype(BF16)
+    ca.prime(8)
+    ca.tick(7)
+    ln_core.wait_recv()
+    r["lns"][...] = r["lnp"][...] + r["lnx"][0]
+
+    def ln_send(delta):
+        return remote(r["lns"], r["lnx"].at[delta], (r["ln_s"], delta), (r["ln_r"], delta), dev(delta))
+
+    for delta in (3, 2, 1):
+        ln_send(delta).start()
     ca.tick(8)
     cb.tick(1)
-    ln_core.wait_recv()
-    r["lns"][...] = r["lnp"][...] + r["lnx"][0]
-
-    def ln_send(delta):
-        return remote(r["lns"], r["lnx"].at[delta], r["ln_s"].at[delta], r["ln_r"].at[delta], dev(delta))
-
-    for delta in (3, 2, 1):
-        ln_send(delta).start()
-    ca.tick(9)
-    cb.tick(2)
     total = r["lns"][...]
     for delta in (1, 2, 3):
         ln_send(delta).wait_recv()
         total += r["lnx"][delta]
     cc.own[0] = total
     cc.prime(0)
+    ca.tick(9)
+    cb.tick(2)
+    cc.tick(1)
     ca.tick(10)
     cb.tick(3)
-    cc.tick(1)
+    cc.tick(2)
     ca.tick(11)
     cb.tick(4)
-    cc.tick(2)
-    r["o_y"][...] = (r["x1"][b] + ys.result()).astype(BF16)
+    cc.tick(3)
     cb.tick(5)
-    cc.tick(3)
     cb.tick(6)
 
     gx.finish(r["x"])
     gdy.finish(r["dy"])
-    gdx.finish(r["dxb"].at[b])
-    gdo.finish(r["dos"].at[chip])
     for at in range(4):
         o_core(at).wait_send()
-    dn.finish()
-    ys.finish()
-    t1_core.wait_send()
-    tq_core.wait_send()
-    d1_core.wait_send()
+    for copy in (t1_core, tp_core, tq_core, dq_core, ln_core, do_core(0)):
+        copy.wait_send()
     for delta in (1, 2, 3):
+        do_send(delta).wait_send()
+        do_core(delta).wait_send()
         t1_send(delta, 0).wait_send()
         t1_send(delta, 1).wait_send()
+        tp_send(delta).wait_send()
         tq_send(delta).wait_send()
-        d1_send(delta).wait_send()
+        dq_send(delta).wait_send()
         ln_send(delta).wait_send()
-    ln_core.wait_send()
     ca.finish()
     cb.finish()
     cc.finish()
+
+
+def widen_kernel(y, gin, gqkv, gproj, gfc1, gfc2, gln, o_y, o_gin, o_qkv, o_proj, o_fc1, o_fc2, *o_ln):
+    o_y[...] = y[...]
+    o_gin[...] = gin[...]
+    o_proj[...] = gproj[...].astype(F32)
+    o_fc1[...] = gfc1[...].astype(F32)
+    o_fc2[...] = gfc2[...].astype(F32)
+    for t in range(3):
+        parts = []
+        for i in range(4):
+            parts.append(gqkv[i, :, 128 * t : 128 * t + 128])
+            parts.append(gqkv[i, :, 384 + 64 * t : 448 + 64 * t])
+        o_qkv[:, 768 * t : 768 * t + 768] = jnp.concatenate(parts, axis=1).astype(F32)
+    for i in range(4):
+        o_ln[i][...] = gln[i, :]
 
 
 def fast_shards(
@@ -859,12 +883,12 @@
     arguments = dict(
         x=(inputs[0], anyspace),
         crops=(crops, smem),
-        ln1_gain=(ln1_gain[None], vmem),
-        ln1_bias=(ln1_bias[None], vmem),
+        ln1_gain=(ln1_gain, vmem),
+        ln1_bias=(ln1_bias, vmem),
         w_qkv=(w_qkv, anyspace),
         w_proj=(w_proj, anyspace),
-        ln2_gain=(ln2_gain[None], vmem),
-        ln2_bias=(ln2_bias[None], vmem),
+        ln2_gain=(ln2_gain, vmem),
+        ln2_bias=(ln2_bias, vmem),
         w_fc1=(w_fc1, anyspace),
         w_fc2=(w_fc2, anyspace),
         dy=(cotangent[0], anyspace),
@@ -876,41 +900,34 @@
         o_proj=((96, 768), BF16),
         o_fc1=((96, 3072), BF16),
         o_fc2=((384, 768), BF16),
-        o_ln=((8, 768), F32),
+        o_ln=((8, 96), F32),
     )
     scratch = dict(
-        ld_sem=D((11,)),
+        ld_sem=D((6,)),
         perm=pltpu.SMEM((8,), jnp.int32),
         inv=pltpu.SMEM((8,), jnp.int32),
-        xb=V((8, 128, 768), BF16), gx_s=D((8,)), gx_r=D((8,)),
-        dyb=V((8, 128, 768), BF16), gdy_s=D((8,)), gdy_r=D((8,)),
-        dxb=V((8, 128, 768), BF16), gdx_s=D((8,)), gdx_r=D((8,)),
-        dob=V((8, 128, 192), BF16), dos=V((4, 128, 192), BF16), gdo_s=D((8,)), gdo_r=D((8,)),
-        wf=V((768, 1152), BF16), w4=V((3, 768, 256), BF16), wo=V((768, 576), BF16),
-        wp=V((768, 768), BF16), w1=V((768, 384), BF16), w2=V((384, 768), BF16),
-        n1=V((8, 128, 768), BF16), n1s=V((512, 768), BF16), qkv=V((8, 128, 1152), BF16),
+        xb=V((8, 128, 768), BF16), gx_s=D((9,)), gx_r=D((9,)),
+        dyb=V((8, 128, 768), BF16), gdy_s=D((9,)), gdy_r=D((9,)),
+        dob=V((8, 128, 192), BF16), dos=V((4, 128, 192), BF16), do_s=D((8,)), do_r=D((8,)),
+        wq=V((768, 2304), BF16), wo=V((4, 768, 576), BF16), wp=V((768, 768), BF16),
+        w1=V((768, 3072), BF16), w2=V((3072, 768), BF16),
+        n1=V((8, 128, 768), BF16), n1s=V((4, 128, 768), BF16), qkv=V((8, 128, 1152), BF16),
         ob=V((2, 8, 128, 384), BF16), o_s=D((4,)), o_r=D((4,)),
         x1=V((8, 128, 768), F32), n2=V((8, 128, 768), BF16),
-        act=V((8, 128, 384), BF16), du=V((8, 128, 384), BF16), part=V((2, 128, 768), F32),
-        dx1=V((128, 768), F32),
+        act=V((8, 128, 384), BF16), slope=V((8, 128, 384), F32), du=V((8, 128, 384), BF16),
+        y=V((128, 768), F32), dn2=V((128, 768), F32), dx1=V((128, 768), F32),
         t1=V((2, 4, 96, 384), BF16), t1x=V((4, 96, 384), BF16),
         t1_cs=D, t1_cr=D, t1_s=D((8,)), t1_r=D((8,)),
-        qo=V((2, 256, 576), BF16), dq=V((2, 256, 576), BF16),
+        tp=V((2, 4, 96, 768), BF16), tpx=V((4, 96, 768), BF16), tps=V((4, 96, 768), BF16), tpr=V((4, 96, 768), BF16),
+        tp_cs=D, tp_cr=D, tp_s=D((4,)), tp_r=D((4,)),
+        qo=V((2, 256, 576), BF16), dq=V((8, 128, 576), BF16),
         tq=V((2, 4, 96, 576), BF16), tqx=V((4, 96, 576), BF16), tqs=V((4, 96, 576), BF16),
         tq_cs=D, tq_cr=D, tq_s=D((4,)), tq_r=D((4,)),
-        d1=V((8, 128, 768), BF16), d1s=V((4, 128, 768), BF16), d1r=V((4, 128, 768), BF16),
-        d1_cs=D, d1_cr=D, d1_s=D((4,)), d1_r=D((4,)),
-        lnp=V((8, 768), F32), lns=V((8, 768), F32), lnx=V((4, 8, 768), F32), ln_s=D((4,)), ln_r=D((4,)),
-    )
-    for name in ("dn", "ys"):
-        scratch.update(
-            {
-                name + "_ctx": V((4, 128, 768), BF16), name + "_crx": V((4, 128, 768), BF16),
-                name + "_keep": V((4, 128, 768), F32), name + "_tx": V((3, 128, 768), BF16),
-                name + "_rx": V((3, 128, 768), BF16), name + "_cs": D((4,)), name + "_cr": D((4,)),
-                name + "_ss": D((3,)), name + "_sr": D((3,)),
-            }
-        )
+        dqs=V((4, 128, 576), BF16), dqr=V((4, 128, 576), BF16),
+        dq_cs=D, dq_cr=D, dq_s=D((4,)), dq_r=D((4,)),
+        lnp=V((8, 768), F32), lns=V((8, 768), F32), lnx=V((4, 8, 768), F32), lnc=V((8, 8, 96), F32),
+        ln_s=D((4,)), ln_r=D((4,)),
+    )
     for name, K, shape, dtype in (
         ("ca", 9, (2, 96, 384), BF16), ("cb", 4, (96, 576), BF16), ("cc", 1, (8, 768), F32)
     ):
@@ -919,7 +936,7 @@
         for part in ("su", "sd", "ru", "rd"):
             scratch[name + "_" + part] = D((K,))
     names = (*arguments, *results, *scratch)
-    y, gin, gqkv, gproj, gfc1, gfc2, gln = pl.pallas_call(
+    narrow = pl.pallas_call(
         functools.partial(layer_kernel, Z, names),
         out_shape=[jax.ShapeDtypeStruct(*shape) for shape in results.values()],
         in_specs=[spec for _, spec in arguments.values()],
@@ -929,12 +946,16 @@
             collective_id=0, has_side_effects=True, vmem_limit_bytes=60 * 2**20
         ),
     )(*[array for array, _ in arguments.values()])
-    gqkv = gqkv.reshape(4, 96, 3, 192).transpose(1, 2, 0, 3).reshape(96, 2304)
-    mine = lax.dynamic_slice_in_dim(gln, 96 * lax.axis_index("blk"), 96, 1)
-    return (
-        y[None], gin[None], gqkv.astype(F32), gproj.astype(F32), gfc1.astype(F32), gfc2.astype(F32),
-        mine[0], mine[1], mine[2], mine[3],
-    )
+    wide = [((128, 768), BF16), ((128, 768), BF16), ((96, 2304), F32), ((96, 768), F32), ((96, 3072), F32), ((384, 768), F32)]
+    wide += [((96,), F32)] * 4
+    y, gin, *grads = pl.pallas_call(
+        widen_kernel,
+        out_shape=[jax.ShapeDtypeStruct(*shape) for shape in wide],
+        in_specs=[vmem] * len(narrow),
+        out_specs=[vmem] * len(wide),
+        compiler_params=pltpu.CompilerParams(vmem_limit_bytes=30 * 2**20),
+    )(*narrow)
+    return (y[None], gin[None], *grads)
 
 
 def solution(mesh):

time: 127 us -> 112 us (0.88)
  Pallas kernels: 111 us -> 105 us
  local copies, waits for them, and re-layouts: 11.6 us -> 6.59 us
  other arithmetic: 2.94 us -> 0 us
    pallas_call x1, Pallas kernels: 111 us -> 103 us  [fast_shards(): pl.pallas_call(functools.partial(layer_kernel, Z, names), out_shape=[jax....]
    unnamed x12 -> x14, local copies, waits for them, and re-layouts: 1.45 us -> 6.59 us
    broadcast_in_dim x4 -> x0, local copies, waits for them, and re-layouts: 5.07 us -> none  [the longest x1 1.27 us: fast_shards(): ln1_gain[None]]
    convert_element_type x3 -> x0, local copies, waits for them, and re-layouts: 3.77 us -> none  [fast_shards(): gqkv.astype(F32)]
    convert_element_type x3 -> x0, other arithmetic: 2.94 us -> none  [the longest x1 1.11 us: fast_shards(): gfc1.astype(F32)]
    pallas_call x0 -> x1, Pallas kernels: none -> 2.03 us  [fast_shards(): pl.pallas_call(widen_kernel, out_shape=[jax.ShapeDtypeStruct(*shape) for...]
where the time goes in v2:
time: 112 us
  Pallas kernels  105 us (94%)
  local copies, waits for them, and re-layouts  6.59 us (6%)
    pallas_call x1, Pallas kernels, fast_shards(): pl.pallas_call(functools.partial(layer_kernel, Z, names), out_shape=[jax....  103 us
    unnamed x14, local copies, waits for them, and re-layouts  6.59 us

profile of v2, /device:TPU:0, one launch (start us, length us, event | category | flops | bytes accessed | tf_op | source)
XLA Modules:
  0.0 112.1 jit_solution(8405699035714470254)
XLA Ops:
  0.6 102.8 %shard_map.186 = (bf16[128,768]{1,0:T(8,128)(2,1)}, bf16[128,768]{1,0:T(8,128)(2,1)}, bf16[4,96,576]{2,1,0:T(8,128)(2,1)}, bf16[96,768]{1,0:T(8,128)(2,1)}, bf16...) custom-call(bf16[128,768]{1,0:T(8,128)(2,1)} %bitcast.4, s32[1,1024]{1,0:T(1,128)} %refs_1_.1, ...), custom_call_target="tpu_custom_call" | custom-call | tf_op jit(solution)/shard_map/pallas_call | solution.py:939
  103.5 0.0 copy-start
  103.5 1.1 copy-done
  104.5 0.0 copy-start.1
  104.5 1.1 copy-done.1
  105.6 0.0 copy-start.2
  105.6 1.0 copy-done.2
  106.6 0.0 copy-start.3
  106.6 0.9 copy-done.3
  107.5 0.0 copy-start.4
  107.5 0.9 copy-done.4
  108.5 0.0 copy-start.5
  108.5 0.9 copy-done.5
  109.4 0.0 copy-start.6
  109.4 0.7 copy-done.6
  110.1 2.0 %shard_map.187 = (bf16[128,768]{1,0:T(8,128)(2,1)}, bf16[128,768]{1,0:T(8,128)(2,1)}, f32[96,2304]{1,0:T(8,128)}, f32[96,768]{1,0:T(8,128)}, f32[96,3072]{1,0:T(...) custom-call(bf16[128,768]{1,0:T(8,128)(2,1)S(1)} %copy-done.3, ...), custom_call_target="tpu_custom_call" | custom-call | tf_op jit(solution)/shard_map/pallas_call | solution.py:951
Async XLA Ops:
  103.5 1.1 copy-start
  104.5 1.1 copy-start.1
  105.6 1.0 copy-start.2
  106.6 0.9 copy-start.3
  107.5 0.9 copy-start.4
  108.5 0.9 copy-start.5
  109.4 0.7 copy-start.6

commit v3 on v2

--- a/solution.py
+++ b/solution.py
@@ -262,6 +262,7 @@
 BF16 = jnp.bfloat16
 RUN_ROWS = 128
 HEAD = 64
+SKEW = 3
 
 
 def mm(left, right):
@@ -432,37 +433,34 @@
                 self.down(self.own.at[k], k).start()
 
         def tick(self, i):
-            ku = i - z
-
-            @pl.when((z > 0) & (ku >= 0) & (ku < self.K))
+            ku = i - 1 - SKEW * (z - 1)
+
+            @pl.when((z > 0) & (z < Z - 1) & (ku >= 0) & (ku < self.K))
             def _():
                 self.up(self.own.at[ku], ku).wait_recv()
-
-                @pl.when(z < Z - 1)
-                def _():
-                    self.tu[ku] = (self.own[ku].astype(F32) + self.rl[ku].astype(F32)).astype(self.dtype)
-                    self.up(self.tu.at[ku], ku).start()
-
-            kd = i - (Z - 1 - z)
-
-            @pl.when((z < Z - 1) & (kd >= 0) & (kd < self.K))
+                self.tu[ku] = (self.own[ku].astype(F32) + self.rl[ku].astype(F32)).astype(self.dtype)
+                self.up(self.tu.at[ku], ku).start()
+
+            kd = i - 1 - SKEW * (Z - 2 - z)
+
+            @pl.when((z > 0) & (z < Z - 1) & (kd >= 0) & (kd < self.K))
             def _():
                 self.down(self.own.at[kd], kd).wait_recv()
-
-                @pl.when(z > 0)
-                def _():
-                    self.td[kd] = (self.own[kd].astype(F32) + self.rr[kd].astype(F32)).astype(self.dtype)
-                    self.down(self.td.at[kd], kd).start()
-
-            k = i - (Z - 1)
+                self.td[kd] = (self.own[kd].astype(F32) + self.rr[kd].astype(F32)).astype(self.dtype)
+                self.down(self.td.at[kd], kd).start()
+
+            k = i - 1 - SKEW * max(Z - 2, 0)
             if 0 <= k < self.K:
 
                 @pl.when(z == 0)
                 def _():
+                    if Z > 1:
+                        self.down(self.own.at[k], k).wait_recv()
                     self.sink(k, self.own[k].astype(F32) + self.rr[k].astype(F32))
 
-                @pl.when(z == Z - 1)
+                @pl.when((z == Z - 1) & (z > 0))
                 def _():
+                    self.up(self.own.at[k], k).wait_recv()
                     self.sink(k, self.own[k].astype(F32) + self.rl[k].astype(F32))
 
                 @pl.when((z > 0) & (z < Z - 1))
@@ -485,28 +483,36 @@
 
     def sink_a(k, total):
         low = total.astype(BF16)
-        if k < 4:
-            r["o_fc2"][96 * k : 96 * k + 96, 0:384] = low[0]
-            r["o_fc2"][96 * k : 96 * k + 96, 384:768] = low[1]
-        elif k < 8:
-            src = chip_at(k - 4)
-            r["o_fc1"][:, pl.ds(pl.multiple_of(768 * src, 128), 384)] = low[0]
-            r["o_fc1"][:, pl.ds(pl.multiple_of(768 * src + 384, 128), 384)] = low[1]
+        if k < 8:
+            r["o_fc2"][96 * (k // 2) : 96 * (k // 2) + 96, 384 * (k % 2) : 384 * (k % 2) + 384] = low
         else:
-            r["o_proj"][:, 0:384] = low[0]
-            r["o_proj"][:, 384:768] = low[1]
+            src = chip_at((k - 8) // 2)
+            r["o_fc1"][:, pl.ds(pl.multiple_of(768 * src + 384 * (k % 2), 128), 384)] = low
 
     def sink_b(k, total):
         r["o_qkv"][chip_at(k)] = total.astype(BF16)
+
+    def sink_p(k, total):
+        r["o_proj"][:, 384 * k : 384 * k + 384] = total.astype(BF16)
 
     def sink_c(k, total):
         for i in range(8):
             r["lnc"][i] = total[:, 96 * i : 96 * i + 96]
         r["o_ln"][...] = r["lnc"][b]
 
-    ca = Chain("ca", 9, BF16, sink_a)
+    ca = Chain("ca", 16, BF16, sink_a)
     cb = Chain("cb", 4, BF16, sink_b)
+    cp = Chain("cp", 2, BF16, sink_p)
     cc = Chain("cc", 1, F32, sink_c)
+    line = ((ca, 0), (cb, 16), (cp, 20), (cc, 22))
+    beats = [0]
+
+    def beat(count=1):
+        for _ in range(count):
+            beats[0] += 1
+            for chain, first in line:
+                if 1 <= beats[0] - first <= chain.K + SKEW * max(Z - 2, 0):
+                    chain.tick(beats[0] - first)
 
     gx.send(r["x"])
 
@@ -612,15 +618,15 @@
         r["slope"][pair] = slope.reshape(2, 128, 384)
         return carry
 
-    lax.fori_loop(0, 4, feed, 0)
+    for c in range(4):
+        feed(c, 0)
     gdy.pass_diagonal()
     for delta in range(4):
         gdy.wait_core(delta)
 
     grad = mm_tn(r["act"][...].reshape(1024, 384), r["dyb"][...].reshape(1024, 768)).astype(BF16)
-    for k in range(4):
-        ca.own[k, 0] = grad[96 * k : 96 * k + 96, 0:384]
-        ca.own[k, 1] = grad[96 * k : 96 * k + 96, 384:768]
+    for k in range(8):
+        ca.own[k] = grad[96 * (k // 2) : 96 * (k // 2) + 96, 384 * (k % 2) : 384 * (k % 2) + 384]
         ca.prime(k)
 
     n2_own = r["n2"][b]
@@ -629,14 +635,17 @@
     r["dn2"][...] = jnp.zeros((128, 768), F32)
 
     def own_rows(i, carry):
-        part = pl.ds(pl.multiple_of(768 * i, 128), 768)
+        part = pl.ds(768 * i, 768)
         act, slope = gelu_pair(mm(r["n2"][b], r["w1"][:, part]))
         du = (mm_nt(r["dyb"][b], r["w2"][part]) * slope).astype(BF16)
         r["dn2"][...] += mm_nt(du, r["w1"][:, part])
         r["y"][...] += mm(act.astype(BF16), r["w2"][part])
         return carry
 
-    lax.fori_loop(0, 4, own_rows, 0)
+    for i in range(4):
+        own_rows(i, 0)
+        if i == 3:
+            beat()
     r["o_y"][...] = r["y"][...].astype(BF16)
 
     dn2 = r["dn2"][...]
@@ -664,7 +673,6 @@
         do_send(delta).start()
     do_core(0).start()
     r["dob"][b] = r["dos"][chip]
-    ca.tick(1)
 
     def back_hidden(c, carry):
         pair = pl.ds(2 * c, 2)
@@ -672,18 +680,20 @@
         r["du"][pair] = (da * r["slope"][pair].reshape(256, 384)).astype(BF16).reshape(2, 128, 384)
         return carry
 
-    lax.fori_loop(0, 4, back_hidden, 0)
+    for c in range(4):
+        back_hidden(c, 0)
     grad = mm_tn(r["n2"][...].reshape(1024, 768), r["du"][...].reshape(1024, 384)).astype(BF16)
     for i in range(8):
         r["t1"][i % 2, i // 2] = grad[96 * i : 96 * i + 96]
     t1_core = remote(r["t1"].at[1 - e], r["t1x"], r["t1_cs"], r["t1_cr"], other)
     t1_core.start()
+    beat()
 
     def t1_send(delta, half):
         src = r["t1"].at[e, chip_at(delta)] if half == 0 else r["t1x"].at[chip_at(delta)]
         hidden_core = e if half == 0 else 1 - e
         at = 2 * delta + half
-        return remote(src, ca.own.at[4 + delta, hidden_core], (r["t1_s"], at), (r["t1_r"], at), dev(delta))
+        return remote(src, ca.own.at[8 + 2 * delta + hidden_core], (r["t1_s"], at), (r["t1_r"], at), dev(delta))
 
     grad = mm_tn(o_rows(b), low).astype(BF16)
     for i in range(8):
@@ -697,7 +707,6 @@
     for s in range(4):
         r["n1s"][s] = r["n1"][r["perm"][4 * e + s]]
     r["qo"][...] = mm(r["n1s"][...].reshape(512, 768), r["wo"][chip]).astype(BF16).reshape(2, 256, 576)
-    ca.tick(2)
 
     for delta in (1, 2, 3):
         do_send(delta).wait_recv()
@@ -706,9 +715,11 @@
     for delta in (1, 2, 3):
         for half in (0, 1):
             t1_send(delta, half).start()
-    ca.own[4, e] = r["t1"][e, chip]
-    ca.own[4, 1 - e] = r["t1x"][chip]
-    ca.prime(4)
+    ca.own[8 + e] = r["t1"][e, chip]
+    ca.own[9 - e] = r["t1x"][chip]
+    ca.prime(8)
+    ca.prime(9)
+    beat()
     for delta in range(4):
         at = do_slot(2 * delta + 1)
         remote(r["dob"].at[at], r["dob"].at[at], (r["do_s"], 2 * delta + 1), (r["do_r"], 2 * delta + 1), other).wait_recv()
@@ -739,9 +750,11 @@
             r["dq"][mine, :, first + wide * t : first + wide * t + wide] = part.astype(BF16).reshape(2, 128, wide)
 
     attend_back(0, 2)
+    beat()
     attend_back(0, 1)
-    ca.tick(3)
+    beat()
     attend_back(1, 2)
+    beat()
     attend_back(1, 1)
 
     dq_core = remote(r["dq"].at[pl.ds(4 * e, 4)], r["dq"].at[pl.ds(4 * e, 4)], r["dq_cs"], r["dq_cr"], other)
@@ -758,7 +771,14 @@
     def dq_send(delta):
         return remote(r["dqs"].at[delta], r["dqr"].at[delta], (r["dq_s"], delta), (r["dq_r"], delta), dev(delta))
 
-    ca.tick(4)
+    beat()
+
+    def t1_arrive(delta):
+        for half in (0, 1):
+            t1_send(delta, half).wait_recv()
+        ca.prime(8 + 2 * delta)
+        ca.prime(9 + 2 * delta)
+
     tq_core.wait_recv()
     for delta in (3, 2, 1, 0):
         c = chip_at(delta)
@@ -768,11 +788,17 @@
         else:
             r["tqs"][delta] = total
             tq_send(delta).start()
+    beat()
+    t1_arrive(1)
     at = pl.ds(4 - 4 * e, 4)
     remote(r["dq"].at[at], r["dq"].at[at], r["dq_cs"], r["dq_cr"], other).wait_recv()
     for delta in (3, 2, 1):
         r["dqs"][delta] = r["dq"][r["inv"][2 * chip_at(delta) + e]]
         dq_send(delta).start()
+    t1_arrive(2)
+    beat()
+    t1_arrive(3)
+    cb.prime(0)
     tp_core.wait_recv()
     for delta in (3, 2, 1, 0):
         c = chip_at(delta)
@@ -780,16 +806,14 @@
         if delta > 0:
             tp_send(delta).start()
 
-    for delta in (1, 2, 3):
-        for half in (0, 1):
-            t1_send(delta, half).wait_recv()
-        ca.prime(4 + delta)
-    ca.tick(5)
-    cb.prime(0)
+    def beat_to(count):
+        beat(count - beats[0])
+
+    beat_to(14)
     for delta in (1, 2, 3):
         tq_send(delta).wait_recv()
         cb.prime(delta)
-    ca.tick(6)
+    beat_to(18)
     dn1 = mm_nt(r["dq"][r["inv"][b]], r["wo"][chip])
     for delta in (1, 2, 3):
         dq_send(delta).wait_recv()
@@ -805,10 +829,9 @@
     for delta in (1, 2, 3):
         tp_send(delta).wait_recv()
         total += r["tpr"][delta].astype(F32)
-    ca.own[8, 0] = total[:, 0:384].astype(BF16)
-    ca.own[8, 1] = total[:, 384:768].astype(BF16)
-    ca.prime(8)
-    ca.tick(7)
+    for k in range(2):
+        cp.own[k] = total[:, 384 * k : 384 * k + 384].astype(BF16)
+        cp.prime(k)
     ln_core.wait_recv()
     r["lns"][...] = r["lnp"][...] + r["lnx"][0]
 
@@ -817,25 +840,14 @@
 
     for delta in (3, 2, 1):
         ln_send(delta).start()
-    ca.tick(8)
-    cb.tick(1)
+    beat_to(20)
     total = r["lns"][...]
     for delta in (1, 2, 3):
         ln_send(delta).wait_recv()
         total += r["lnx"][delta]
     cc.own[0] = total
     cc.prime(0)
-    ca.tick(9)
-    cb.tick(2)
-    cc.tick(1)
-    ca.tick(10)
-    cb.tick(3)
-    cc.tick(2)
-    ca.tick(11)
-    cb.tick(4)
-    cc.tick(3)
-    cb.tick(5)
-    cb.tick(6)
+    beat_to(23 + SKEW * max(Z - 2, 0))
 
     gx.finish(r["x"])
     gdy.finish(r["dy"])
@@ -854,23 +866,46 @@
         ln_send(delta).wait_send()
     ca.finish()
     cb.finish()
+    cp.finish()
     cc.finish()
 
 
-def widen_kernel(y, gin, gqkv, gproj, gfc1, gfc2, gln, o_y, o_gin, o_qkv, o_proj, o_fc1, o_fc2, *o_ln):
-    o_y[...] = y[...]
-    o_gin[...] = gin[...]
-    o_proj[...] = gproj[...].astype(F32)
-    o_fc1[...] = gfc1[...].astype(F32)
-    o_fc2[...] = gfc2[...].astype(F32)
-    for t in range(3):
-        parts = []
-        for i in range(4):
-            parts.append(gqkv[i, :, 128 * t : 128 * t + 128])
-            parts.append(gqkv[i, :, 384 + 64 * t : 448 + 64 * t])
-        o_qkv[:, 768 * t : 768 * t + 768] = jnp.concatenate(parts, axis=1).astype(F32)
-    for i in range(4):
-        o_ln[i][...] = gln[i, :]
+def widen_kernel(*refs):
+    sources, results, held, wide = refs[:7], refs[7:17], refs[17:24], refs[24:32]
+    sem_in, sem_out = refs[32:]
+    order = (4, 5, 2, 3, 6, 0, 1)
+    copies = {i: pltpu.make_async_copy(sources[i], held[i], sem_in.at[i]) for i in order}
+    for copy in copies.values():
+        copy.start()
+    leaving = []
+
+    def leave(src, at):
+        copy = pltpu.make_async_copy(src, results[at], sem_out.at[at])
+        copy.start()
+        leaving.append(copy)
+
+    for i in order:
+        copies[i].wait()
+        part = held[i]
+        if i < 2:
+            leave(part, i)
+        elif i == 2:
+            for t in range(3):
+                parts = []
+                for c in range(4):
+                    parts.append(part[c, :, 128 * t : 128 * t + 128])
+                    parts.append(part[c, :, 384 + 64 * t : 448 + 64 * t])
+                wide[0][:, 768 * t : 768 * t + 768] = jnp.concatenate(parts, axis=1).astype(F32)
+            leave(wide[0], 2)
+        elif i < 6:
+            wide[i - 2][...] = part[...].astype(F32)
+            leave(wide[i - 2], i)
+        else:
+            for t in range(4):
+                wide[4 + t][...] = part[t, :]
+                leave(wide[4 + t], 6 + t)
+    for copy in leaving:
+        copy.wait()
 
 
 def fast_shards(
@@ -929,7 +964,7 @@
         ln_s=D((4,)), ln_r=D((4,)),
     )
     for name, K, shape, dtype in (
-        ("ca", 9, (2, 96, 384), BF16), ("cb", 4, (96, 576), BF16), ("cc", 1, (8, 768), F32)
+        ("ca", 16, (96, 384), BF16), ("cb", 4, (96, 576), BF16), ("cp", 2, (96, 384), BF16), ("cc", 1, (8, 768), F32)
     ):
         for part in ("own", "rl", "rr", "tu", "td"):
             scratch[name + "_" + part] = V((K, *shape), dtype)
@@ -951,9 +986,13 @@
     y, gin, *grads = pl.pallas_call(
         widen_kernel,
         out_shape=[jax.ShapeDtypeStruct(*shape) for shape in wide],
-        in_specs=[vmem] * len(narrow),
-        out_specs=[vmem] * len(wide),
-        compiler_params=pltpu.CompilerParams(vmem_limit_bytes=30 * 2**20),
+        in_specs=[anyspace] * len(narrow),
+        out_specs=[anyspace] * len(wide),
+        scratch_shapes=[V(*shape) for shape in results.values()]
+        + [V(*shape) for shape in wide[2:6]]
+        + [V((96,), F32)] * 4
+        + [D((len(narrow),)), D((len(wide),))],
+        compiler_params=pltpu.CompilerParams(vmem_limit_bytes=62 * 2**20),
     )(*narrow)
     return (y[None], gin[None], *grads)
 

time: 112 us -> 93.5 us (0.83)
  Pallas kernels: 105 us -> 92.5 us
  local copies, waits for them, and re-layouts: 6.59 us -> 0 us
    pallas_call x1, Pallas kernels: 103 us -> 89.3 us  [fast_shards(): pl.pallas_call(functools.partial(layer_kernel, Z, names), out_shape=[jax....]
    unnamed x14 -> x0, local copies, waits for them, and re-layouts: 6.59 us -> none
    pallas_call x1, Pallas kernels: 2.03 us -> 3.22 us  [fast_shards(): pl.pallas_call(widen_kernel, out_shape=[jax.ShapeDtypeStruct(*shape) for...]
where the time goes in v3:
time: 93.5 us; the launch traced here: 93.3 us
  Pallas kernels  92.5 us (99%)
    pallas_call x1, Pallas kernels, fast_shards(): pl.pallas_call(functools.partial(layer_kernel, Z, names), out_shape=[jax....  89.3 us
    pallas_call x1, Pallas kernels, fast_shards(): pl.pallas_call(widen_kernel, out_shape=[jax.ShapeDtypeStruct(*shape) for...  3.22 us

profile of v3, /device:TPU:0, one launch (start us, length us, event | category | flops | bytes accessed | tf_op | source)
XLA Modules:
  0.0 93.3 jit_solution(17674213546332446750)
XLA Ops:
  0.6 89.3 %shard_map.186 = (bf16[128,768]{1,0:T(8,128)(2,1)}, bf16[128,768]{1,0:T(8,128)(2,1)}, bf16[4,96,576]{2,1,0:T(8,128)(2,1)}, bf16[96,768]{1,0:T(8,128)(2,1)}, bf16...) custom-call(bf16[128,768]{1,0:T(8,128)(2,1)} %bitcast.4, s32[1,1024]{1,0:T(1,128)} %refs_1_.1, ...), custom_call_target="tpu_custom_call" | custom-call | tf_op jit(solution)/shard_map/pallas_call | solution.py:974
  89.9 3.2 %shard_map.187 = (bf16[128,768]{1,0:T(8,128)(2,1)}, bf16[128,768]{1,0:T(8,128)(2,1)}, f32[96,2304]{1,0:T(8,128)}, f32[96,768]{1,0:T(8,128)}, f32[96,3072]{1,0:T(...) custom-call(bf16[128,768]{1,0:T(8,128)(2,1)} %get-tuple-element.27.refs_0_, ...), custom_call_target="tpu_custom_call" | custom-call | tf_op jit(solution)/shard_map/pallas_call | solution.py:986

commit v4 on v3

--- a/solution.py
+++ b/solution.py
@@ -333,11 +333,6 @@
         loads[name].start()
 
     load("x", r["x"], r["xb"].at[b])
-    load("w_qkv", r["w_qkv"], r["wq"])
-    load("w_proj", r["w_proj"], r["wp"])
-    load("dy", r["dy"], r["dyb"].at[b])
-    load("w_fc1", r["w_fc1"], r["w1"])
-    load("w_fc2", r["w_fc2"], r["w2"])
 
     bar = pltpu.get_barrier_semaphore()
     for target in (other, dev(1), dev(2), dev(3)):
@@ -360,50 +355,64 @@
         def slot(self, m):
             return 2 * chip_at(m // 2) + (e if m % 2 == 0 else 1 - e)
 
-        def hop(self, delta, src=None):
-            at = b if src is not None else self.slot(2 * delta)
-            src = self.buf.at[at] if src is None else src
-            return remote(src, self.buf.at[at], (self.ss, 2 * delta), (self.rs, 2 * delta), dev(delta))
-
-        def half(self, part, delta, towards):
+        def copy(self, src, at, place, device):
+            return remote(src, self.buf.at[at], (self.ss, place), (self.rs, place), device)
+
+        def hop(self, delta, part, src=None):
+            rows = pl.ds(64 * part, 64)
+            at = (self.slot(2 * delta) if src is None else b, rows)
+            return self.copy(self.buf.at[at] if src is None else src.at[rows], at, 2 * delta + part, dev(delta))
+
+        def turn(self, part, delta):
             at = (self.slot(2 * delta), pl.ds(64 * part, 64))
-            return remote(self.buf.at[at], self.buf.at[at], (self.ss, 6 + 2 * part), (self.rs, 6 + 2 * part), dev(towards))
+            return self.copy(self.buf.at[at], at, 6 + part, dev(2 - part))
 
         def core(self, delta, src=None):
-            at = b if src is not None else self.slot(2 * delta)
-            src = self.buf.at[at] if src is None else src
-            return remote(src, self.buf.at[at], (self.ss, 2 * delta + 1), (self.rs, 2 * delta + 1), other)
+            at = self.slot(2 * delta) if src is None else b
+            return self.copy(self.buf.at[at] if src is None else src, at, (0, 8, 9)[delta], other)
+
+        def core_half(self, part):
+            at = (self.slot(6), pl.ds(64 * part, 64))
+            return self.copy(self.buf.at[at], at, 10 + part, other)
 
         def send(self, src):
-            self.hop(1, src).start()
-            self.hop(2, src).start()
+            for part in (0, 1):
+                self.hop(1, part, src).start()
+                self.hop(2, 1 - part, src).start()
             self.core(0, src).start()
 
         def pass_on(self):
-            self.hop(1).wait_recv()
-            self.half(0, 1, 2).start()
-            self.hop(2).wait_recv()
-            self.half(1, 2, 1).start()
+            self.hop(1, 0).wait_recv()
+            self.turn(0, 1).start()
+            self.hop(2, 1).wait_recv()
+            self.turn(1, 2).start()
+            self.hop(1, 1).wait_recv()
             self.core(1).start()
+            self.hop(2, 0).wait_recv()
             self.core(2).start()
 
         def pass_diagonal(self):
-            self.half(0, 3, 2).wait_recv()
-            self.half(1, 3, 1).wait_recv()
-            self.core(3).start()
+            for part in (0, 1):
+                self.turn(part, 3).wait_recv()
+                self.core_half(part).start()
 
         def wait_core(self, delta):
             at = self.slot(2 * delta + 1)
-            remote(self.buf.at[at], self.buf.at[at], (self.ss, 2 * delta + 1), (self.rs, 2 * delta + 1), other).wait_recv()
+            if delta < 3:
+                self.copy(self.buf.at[at], at, (0, 8, 9)[delta], other).wait_recv()
+            else:
+                for part in (0, 1):
+                    half = (at, pl.ds(64 * part, 64))
+                    self.copy(self.buf.at[half], half, 10 + part, other).wait_recv()
 
         def finish(self, src):
-            self.hop(1, src).wait_send()
-            self.hop(2, src).wait_send()
-            self.half(0, 1, 2).wait_send()
-            self.half(1, 2, 1).wait_send()
             self.core(0, src).wait_send()
-            for delta in (1, 2, 3):
-                self.core(delta).wait_send()
+            for part in (0, 1):
+                self.hop(1, part, src).wait_send()
+                self.hop(2, part, src).wait_send()
+                self.turn(part, 1 + part).wait_send()
+                self.core(1 + part).wait_send()
+                self.core_half(part).wait_send()
 
     gx = Gather(r["xb"], r["gx_s"], r["gx_r"])
     gdy = Gather(r["dyb"], r["gdy_s"], r["gdy_r"])
@@ -515,6 +524,11 @@
                     chain.tick(beats[0] - first)
 
     gx.send(r["x"])
+    load("w_qkv", r["w_qkv"], r["wq"])
+    load("w_proj", r["w_proj"], r["wp"])
+    load("dy", r["dy"], r["dyb"].at[b])
+    load("w_fc1", r["w_fc1"], r["w1"])
+    load("w_fc2", r["w_fc2"], r["w2"])
 
     crop = [r["crops"][0, RUN_ROWS * i] for i in range(8)]
     places = []
@@ -583,60 +597,61 @@
             ]
             s = mm_nt(stack(q), k)
             p = jnp.exp(s - jnp.max(s, axis=-1, keepdims=True))
-            o = mm(p.astype(BF16), v) / jnp.sum(p, axis=-1, keepdims=True)
+            o = mm(p.astype(BF16), jnp.concatenate([v, jnp.ones_like(v)], axis=1))
+            o = o[:, 0:128] / o[:, 128:256]
             outs.append(jnp.where(low_lanes, o[0:256], o[256:512]))
         low = jnp.concatenate(outs, axis=1).astype(BF16)
         r["ob"][e, pl.ds(2 * at, 2)] = low.reshape(2, 128, 384)
         o_core(at).start()
         return carry
 
-    lax.fori_loop(0, 3, attend, 0)
-    gdy.pass_on()
-    attend(3, 0)
-    for name in ("w_proj", "w_fc1", "w_fc2", "dy"):
-        loads[name].wait()
-    for at in range(4):
+    def by_perm(buf, first, count):
+        return jnp.concatenate([buf[r["perm"][first + i]] for i in range(count)], axis=0)
+
+    own_hidden = pl.ds(pl.multiple_of(384 * b, 128), 384)
+
+    def feed(at):
         place = (1 - e, pl.ds(2 * at, 2))
         remote(r["ob"].at[place], r["ob"].at[place], (r["o_s"], at), (r["o_r"], at), other).wait_recv()
-
-    def o_rows(run):
-        at = r["inv"][run]
-        return jnp.concatenate([r["ob"][0, at], r["ob"][1, at]], axis=1)
-
-    own_hidden = pl.ds(pl.multiple_of(384 * b, 128), 384)
-
-    def feed(c, carry):
-        pair = pl.ds(2 * c, 2)
-        o = jnp.concatenate([o_rows(2 * c), o_rows(2 * c + 1)], axis=0)
-        x1 = r["xb"][pair].reshape(256, 768).astype(F32) + mm(o, r["wp"][...])
+        pair = pl.ds(2 * at, 2)
+        o = jnp.concatenate([r["ob"][i, pair].reshape(256, 384) for i in range(2)], axis=1)
+        x1 = by_perm(r["xb"], 2 * at, 2).astype(F32) + mm(o, r["wp"][...])
         r["x1"][pair] = x1.reshape(2, 128, 768)
         hat, _ = norm_parts(x1)
         n2 = (hat * g2 + b2).astype(BF16)
         r["n2"][pair] = n2.reshape(2, 128, 768)
-        act, slope = gelu_pair(mm(n2, r["w1"][:, own_hidden]))
-        r["act"][pair] = act.astype(BF16).reshape(2, 128, 384)
-        r["slope"][pair] = slope.reshape(2, 128, 384)
-        return carry
-
-    for c in range(4):
-        feed(c, 0)
+        u = mm(n2, r["w1"][:, own_hidden])
+        r["u"][pair] = u.reshape(2, 128, 384)
+        r["act"][pair] = gelu_pair(u)[0].astype(BF16).reshape(2, 128, 384)
+
+    attend(0, 0)
+    attend(1, 0)
+    for name in ("w_proj", "w_fc1", "w_fc2", "dy"):
+        loads[name].wait()
+    gdy.pass_on()
+    feed(0)
+    attend(2, 0)
+    feed(1)
+    attend(3, 0)
     gdy.pass_diagonal()
+    feed(2)
     for delta in range(4):
         gdy.wait_core(delta)
-
-    grad = mm_tn(r["act"][...].reshape(1024, 384), r["dyb"][...].reshape(1024, 768)).astype(BF16)
+    feed(3)
+
+    grad = mm_tn(r["act"][...].reshape(1024, 384), by_perm(r["dyb"], 0, 8)).astype(BF16)
     for k in range(8):
         ca.own[k] = grad[96 * (k // 2) : 96 * (k // 2) + 96, 384 * (k % 2) : 384 * (k % 2) + 384]
         ca.prime(k)
 
-    n2_own = r["n2"][b]
+    place_own = r["inv"][b]
     dy_own = r["dyb"][b]
-    r["y"][...] = r["x1"][b]
+    r["y"][...] = r["x1"][place_own]
     r["dn2"][...] = jnp.zeros((128, 768), F32)
 
     def own_rows(i, carry):
         part = pl.ds(768 * i, 768)
-        act, slope = gelu_pair(mm(r["n2"][b], r["w1"][:, part]))
+        act, slope = gelu_pair(mm(r["n2"][place_own], r["w1"][:, part]))
         du = (mm_nt(r["dyb"][b], r["w2"][part]) * slope).astype(BF16)
         r["dn2"][...] += mm_nt(du, r["w1"][:, part])
         r["y"][...] += mm(act.astype(BF16), r["w2"][part])
@@ -649,7 +664,7 @@
     r["o_y"][...] = r["y"][...].astype(BF16)
 
     dn2 = r["dn2"][...]
-    hat, inv_std = norm_parts(r["x1"][b])
+    hat, inv_std = norm_parts(r["x1"][place_own])
     r["lnp"][2:3] = jnp.sum(dn2 * hat, axis=0, keepdims=True)
     r["lnp"][3:4] = jnp.sum(dn2, axis=0, keepdims=True)
     dx1 = dy_own.astype(F32) + norm_back(dn2, hat, inv_std, g2)
@@ -673,15 +688,18 @@
         do_send(delta).start()
     do_core(0).start()
     r["dob"][b] = r["dos"][chip]
+    beat()
 
     def back_hidden(c, carry):
         pair = pl.ds(2 * c, 2)
-        da = mm_nt(r["dyb"][pair].reshape(256, 768), r["w2"][own_hidden])
-        r["du"][pair] = (da * r["slope"][pair].reshape(256, 384)).astype(BF16).reshape(2, 128, 384)
+        da = mm_nt(by_perm(r["dyb"], 2 * c, 2), r["w2"][own_hidden])
+        slope = gelu_pair(r["u"][pair].reshape(256, 384))[1]
+        r["du"][pair] = (da * slope).astype(BF16).reshape(2, 128, 384)
         return carry
 
     for c in range(4):
         back_hidden(c, 0)
+    beat()
     grad = mm_tn(r["n2"][...].reshape(1024, 768), r["du"][...].reshape(1024, 384)).astype(BF16)
     for i in range(8):
         r["t1"][i % 2, i // 2] = grad[96 * i : 96 * i + 96]
@@ -695,7 +713,8 @@
         at = 2 * delta + half
         return remote(src, ca.own.at[8 + 2 * delta + hidden_core], (r["t1_s"], at), (r["t1_r"], at), dev(delta))
 
-    grad = mm_tn(o_rows(b), low).astype(BF16)
+    o = jnp.concatenate([r["ob"][i, place_own] for i in range(2)], axis=1)
+    grad = mm_tn(o, low).astype(BF16)
     for i in range(8):
         r["tp"][i % 2, i // 2] = grad[96 * i : 96 * i + 96]
     tp_core = remote(r["tp"].at[1 - e], r["tpx"], r["tp_cs"], r["tp_cr"], other)
@@ -704,13 +723,6 @@
     def tp_send(delta):
         return remote(r["tps"].at[delta], r["tpr"].at[delta], (r["tp_s"], delta), (r["tp_r"], delta), dev(delta))
 
-    for s in range(4):
-        r["n1s"][s] = r["n1"][r["perm"][4 * e + s]]
-    r["qo"][...] = mm(r["n1s"][...].reshape(512, 768), r["wo"][chip]).astype(BF16).reshape(2, 256, 576)
-
-    for delta in (1, 2, 3):
-        do_send(delta).wait_recv()
-        do_core(delta).start()
     t1_core.wait_recv()
     for delta in (1, 2, 3):
         for half in (0, 1):
@@ -720,9 +732,19 @@
     ca.prime(8)
     ca.prime(9)
     beat()
+
+    for s in range(4):
+        r["n1s"][s] = r["n1"][r["perm"][4 * e + s]]
+    r["qo"][...] = mm(r["n1s"][...].reshape(512, 768), r["wo"][chip]).astype(BF16).reshape(2, 256, 576)
+
+    for delta in (1, 2, 3):
+        do_send(delta).wait_recv()
+        do_core(delta).start()
     for delta in range(4):
         at = do_slot(2 * delta + 1)
         remote(r["dob"].at[at], r["dob"].at[at], (r["do_s"], 2 * delta + 1), (r["do_r"], 2 * delta + 1), other).wait_recv()
+
+    beat()
 
     def attend_back(at, heads):
         runs = [r["perm"][4 * e + 2 * at + i] for i in range(2)]
@@ -779,6 +801,7 @@
         ca.prime(8 + 2 * delta)
         ca.prime(9 + 2 * delta)
 
+    t1_arrive(1)
     tq_core.wait_recv()
     for delta in (3, 2, 1, 0):
         c = chip_at(delta)
@@ -789,16 +812,11 @@
             r["tqs"][delta] = total
             tq_send(delta).start()
     beat()
-    t1_arrive(1)
     at = pl.ds(4 - 4 * e, 4)
     remote(r["dq"].at[at], r["dq"].at[at], r["dq_cs"], r["dq_cr"], other).wait_recv()
     for delta in (3, 2, 1):
         r["dqs"][delta] = r["dq"][r["inv"][2 * chip_at(delta) + e]]
         dq_send(delta).start()
-    t1_arrive(2)
-    beat()
-    t1_arrive(3)
-    cb.prime(0)
     tp_core.wait_recv()
     for delta in (3, 2, 1, 0):
         c = chip_at(delta)
@@ -809,7 +827,11 @@
     def beat_to(count):
         beat(count - beats[0])
 
-    beat_to(14)
+    t1_arrive(2)
+    beat_to(13)
+    t1_arrive(3)
+    cb.prime(0)
+    beat_to(15)
     for delta in (1, 2, 3):
         tq_send(delta).wait_recv()
         cb.prime(delta)
@@ -825,6 +847,15 @@
     r["o_gin"][...] = (r["dx1"][...] + norm_back(dn1, hat, inv_std, g1)).astype(BF16)
     ln_core = remote(r["lnp"], r["lnx"].at[0], (r["ln_s"], 0), (r["ln_r"], 0), other)
     ln_core.start()
+    beat_to(19)
+    ln_core.wait_recv()
+    r["lns"][...] = r["lnp"][...] + r["lnx"][0]
+
+    def ln_send(delta):
+        return remote(r["lns"], r["lnx"].at[delta], (r["ln_s"], delta), (r["ln_r"], delta), dev(delta))
+
+    for delta in (3, 2, 1):
+        ln_send(delta).start()
     total = r["tps"][0].astype(F32)
     for delta in (1, 2, 3):
         tp_send(delta).wait_recv()
@@ -832,14 +863,6 @@
     for k in range(2):
         cp.own[k] = total[:, 384 * k : 384 * k + 384].astype(BF16)
         cp.prime(k)
-    ln_core.wait_recv()
-    r["lns"][...] = r["lnp"][...] + r["lnx"][0]
-
-    def ln_send(delta):
-        return remote(r["lns"], r["lnx"].at[delta], (r["ln_s"], delta), (r["ln_r"], delta), dev(delta))
-
-    for delta in (3, 2, 1):
-        ln_send(delta).start()
     beat_to(20)
     total = r["lns"][...]
     for delta in (1, 2, 3):
@@ -941,15 +964,15 @@
         ld_sem=D((6,)),
         perm=pltpu.SMEM((8,), jnp.int32),
         inv=pltpu.SMEM((8,), jnp.int32),
-        xb=V((8, 128, 768), BF16), gx_s=D((9,)), gx_r=D((9,)),
-        dyb=V((8, 128, 768), BF16), gdy_s=D((9,)), gdy_r=D((9,)),
+        xb=V((8, 128, 768), BF16), gx_s=D((12,)), gx_r=D((12,)),
+        dyb=V((8, 128, 768), BF16), gdy_s=D((12,)), gdy_r=D((12,)),
         dob=V((8, 128, 192), BF16), dos=V((4, 128, 192), BF16), do_s=D((8,)), do_r=D((8,)),
         wq=V((768, 2304), BF16), wo=V((4, 768, 576), BF16), wp=V((768, 768), BF16),
         w1=V((768, 3072), BF16), w2=V((3072, 768), BF16),
         n1=V((8, 128, 768), BF16), n1s=V((4, 128, 768), BF16), qkv=V((8, 128, 1152), BF16),
         ob=V((2, 8, 128, 384), BF16), o_s=D((4,)), o_r=D((4,)),
         x1=V((8, 128, 768), F32), n2=V((8, 128, 768), BF16),
-        act=V((8, 128, 384), BF16), slope=V((8, 128, 384), F32), du=V((8, 128, 384), BF16),
+        act=V((8, 128, 384), BF16), u=V((8, 128, 384), F32), du=V((8, 128, 384), BF16),
         y=V((128, 768), F32), dn2=V((128, 768), F32), dx1=V((128, 768), F32),
         t1=V((2, 4, 96, 384), BF16), t1x=V((4, 96, 384), BF16),
         t1_cs=D, t1_cr=D, t1_s=D((8,)), t1_r=D((8,)),

time: 93.5 us -> 92 us (0.984)
  Pallas kernels: 92.5 us -> 91 us
    pallas_call x1, Pallas kernels: 89.3 us -> 87.8 us  [fast_shards(): pl.pallas_call(functools.partial(layer_kernel, Z, names), out_shape=[jax....]
where the time goes in v4:
time: 92 us; the launch traced here: 91.8 us
  Pallas kernels  91 us (99%)
    pallas_call x1, Pallas kernels, fast_shards(): pl.pallas_call(functools.partial(layer_kernel, Z, names), out_shape=[jax....  87.8 us
    pallas_call x1, Pallas kernels, fast_shards(): pl.pallas_call(widen_kernel, out_shape=[jax.ShapeDtypeStruct(*shape) for...  3.22 us

profile of v4, /device:TPU:0, one launch (start us, length us, event | category | flops | bytes accessed | tf_op | source)
XLA Modules:
  0.0 91.8 jit_solution(7142048713278752991)
XLA Ops:
  0.6 87.8 %shard_map.186 = (bf16[128,768]{1,0:T(8,128)(2,1)}, bf16[128,768]{1,0:T(8,128)(2,1)}, bf16[4,96,576]{2,1,0:T(8,128)(2,1)}, bf16[96,768]{1,0:T(8,128)(2,1)}, bf16...) custom-call(bf16[128,768]{1,0:T(8,128)(2,1)} %bitcast.4, s32[1,1024]{1,0:T(1,128)} %refs_1_.1, ...), custom_call_target="tpu_custom_call" | custom-call | tf_op jit(solution)/shard_map/pallas_call | solution.py:997
  88.4 3.2 %shard_map.187 = (bf16[128,768]{1,0:T(8,128)(2,1)}, bf16[128,768]{1,0:T(8,128)(2,1)}, f32[96,2304]{1,0:T(8,128)}, f32[96,768]{1,0:T(8,128)}, f32[96,3072]{1,0:T(...) custom-call(bf16[128,768]{1,0:T(8,128)(2,1)} %get-tuple-element.27.refs_0_, ...), custom_call_target="tpu_custom_call" | custom-call | tf_op jit(solution)/shard_map/pallas_call | solution.py:1009

commit v5 on v4

--- a/solution.py
+++ b/solution.py
@@ -262,7 +262,7 @@
 BF16 = jnp.bfloat16
 RUN_ROWS = 128
 HEAD = 64
-SKEW = 3
+SKEW = 2
 
 
 def mm(left, right):
@@ -381,11 +381,13 @@
                 self.hop(2, 1 - part, src).start()
             self.core(0, src).start()
 
-        def pass_on(self):
+        def pass_first(self):
             self.hop(1, 0).wait_recv()
             self.turn(0, 1).start()
             self.hop(2, 1).wait_recv()
             self.turn(1, 2).start()
+
+        def pass_second(self):
             self.hop(1, 1).wait_recv()
             self.core(1).start()
             self.hop(2, 0).wait_recv()
@@ -418,8 +420,8 @@
     gdy = Gather(r["dyb"], r["gdy_s"], r["gdy_r"])
 
     class Chain:
-        def __init__(self, name, K, dtype, sink):
-            self.K, self.dtype, self.sink = K, dtype, sink
+        def __init__(self, name, K, dtype, sink, place):
+            self.K, self.dtype, self.sink, self.place = K, dtype, sink, place
             for part in ("own", "rl", "rr", "tu", "td", "su", "sd", "ru", "rd"):
                 setattr(self, part, r[name + "_" + part])
 
@@ -479,6 +481,8 @@
                         self.own[k].astype(F32) + self.rl[k].astype(F32) + self.rr[k].astype(F32),
                     )
 
+                leave(*self.place(k))
+
         def finish(self):
             @pl.when(z < Z - 1)
             def _():
@@ -490,30 +494,45 @@
                 for k in range(self.K):
                     self.down(self.own.at[k], k).wait_send()
 
-    def sink_a(k, total):
-        low = total.astype(BF16)
+    leaving = []
+
+    def leave(name, at):
+        copy = pltpu.make_async_copy(r["s_" + name].at[at], r["o_" + name].at[at], r["out_sem"].at[len(leaving)])
+        copy.start()
+        leaving.append(copy)
+
+    def place_a(k):
         if k < 8:
-            r["o_fc2"][96 * (k // 2) : 96 * (k // 2) + 96, 384 * (k % 2) : 384 * (k % 2) + 384] = low
-        else:
-            src = chip_at((k - 8) // 2)
-            r["o_fc1"][:, pl.ds(pl.multiple_of(768 * src + 384 * (k % 2), 128), 384)] = low
-
-    def sink_b(k, total):
-        r["o_qkv"][chip_at(k)] = total.astype(BF16)
-
-    def sink_p(k, total):
-        r["o_proj"][:, 384 * k : 384 * k + 384] = total.astype(BF16)
+            return "fc2", (pl.ds(96 * (k // 2), 96), pl.ds(384 * (k % 2), 384))
+        src = chip_at((k - 8) // 2)
+        return "fc1", (slice(None), pl.ds(pl.multiple_of(768 * src + 384 * (k % 2), 128), 384))
+
+    def place_b(k):
+        return "qkv", (chip_at(k),)
+
+    def place_p(k):
+        return "proj", (slice(None), pl.ds(384 * k, 384))
+
+    def sink_to(place):
+        def sink(k, total):
+            name, at = place(k)
+            r["s_" + name][at] = total.astype(BF16)
+
+        return sink
+
+    def place_c(k):
+        return "ln", (slice(None),)
 
     def sink_c(k, total):
         for i in range(8):
             r["lnc"][i] = total[:, 96 * i : 96 * i + 96]
-        r["o_ln"][...] = r["lnc"][b]
-
-    ca = Chain("ca", 16, BF16, sink_a)
-    cb = Chain("cb", 4, BF16, sink_b)
-    cp = Chain("cp", 2, BF16, sink_p)
-    cc = Chain("cc", 1, F32, sink_c)
-    line = ((ca, 0), (cb, 16), (cp, 20), (cc, 22))
+        r["s_ln"][...] = r["lnc"][b]
+
+    ca = Chain("ca", 16, BF16, sink_to(place_a), place_a)
+    cb = Chain("cb", 4, BF16, sink_to(place_b), place_b)
+    cp = Chain("cp", 2, BF16, sink_to(place_p), place_p)
+    cc = Chain("cc", 1, F32, sink_c, place_c)
+    line = ((ca, 0), (cb, 16), (cp, 20))
     beats = [0]
 
     def beat(count=1):
@@ -549,11 +568,6 @@
 
     loads["x"].wait()
     loads["w_qkv"].wait()
-    for i in range(4):
-        for t in range(3):
-            first = 768 * t + 192 * i
-            r["wo"][i, :, 128 * t : 128 * t + 128] = r["wq"][:, first : first + 128]
-            r["wo"][i, :, 384 + 64 * t : 448 + 64 * t] = r["wq"][:, first + 128 : first + 192]
 
     def project(delta):
         gx.wait_core(delta)
@@ -567,8 +581,9 @@
             r["qkv"][pair, :, 384 * t : 384 * t + 384] = out.astype(BF16).reshape(2, 128, 384)
 
     project(0)
-    gx.pass_on()
+    gx.pass_first()
     gdy.send(r["dy"])
+    gx.pass_second()
     project(1)
     project(2)
     gx.pass_diagonal()
@@ -625,19 +640,20 @@
         r["act"][pair] = gelu_pair(u)[0].astype(BF16).reshape(2, 128, 384)
 
     attend(0, 0)
+    gdy.pass_first()
     attend(1, 0)
     for name in ("w_proj", "w_fc1", "w_fc2", "dy"):
         loads[name].wait()
-    gdy.pass_on()
     feed(0)
+    gdy.pass_second()
     attend(2, 0)
     feed(1)
     attend(3, 0)
+    feed(2)
     gdy.pass_diagonal()
-    feed(2)
+    feed(3)
     for delta in range(4):
         gdy.wait_core(delta)
-    feed(3)
 
     grad = mm_tn(r["act"][...].reshape(1024, 384), by_perm(r["dyb"], 0, 8)).astype(BF16)
     for k in range(8):
@@ -661,7 +677,8 @@
         own_rows(i, 0)
         if i == 3:
             beat()
-    r["o_y"][...] = r["y"][...].astype(BF16)
+    r["s_y"][...] = r["y"][...].astype(BF16)
+    leave("y", (slice(None),))
 
     dn2 = r["dn2"][...]
     hat, inv_std = norm_parts(r["x1"][place_own])
@@ -735,7 +752,13 @@
 
     for s in range(4):
         r["n1s"][s] = r["n1"][r["perm"][4 * e + s]]
-    r["qo"][...] = mm(r["n1s"][...].reshape(512, 768), r["wo"][chip]).astype(BF16).reshape(2, 256, 576)
+    odd = lax.rem(chip, 2) == 1
+    for t in range(3):
+        first = pl.multiple_of(768 * t + 192 * chip - 64 * lax.rem(chip, 2), 128)
+        four = mm(r["n1s"][...].reshape(512, 768), r["wq"][:, pl.ds(first, 256)])
+        three = jnp.where(odd, four[:, 64:256], four[:, 0:192]).astype(BF16)
+        r["qo"][:, :, 128 * t : 128 * t + 128] = three[:, 0:128].reshape(2, 256, 128)
+        r["qo"][:, :, 384 + 64 * t : 448 + 64 * t] = three[:, 128:192].reshape(2, 256, 64)
 
     for delta in (1, 2, 3):
         do_send(delta).wait_recv()
@@ -745,6 +768,12 @@
         remote(r["dob"].at[at], r["dob"].at[at], (r["do_s"], 2 * delta + 1), (r["do_r"], 2 * delta + 1), other).wait_recv()
 
     beat()
+
+    def t1_arrive(delta):
+        for half in (0, 1):
+            t1_send(delta, half).wait_recv()
+        ca.prime(8 + 2 * delta)
+        ca.prime(9 + 2 * delta)
 
     def attend_back(at, heads):
         runs = [r["perm"][4 * e + 2 * at + i] for i in range(2)]
@@ -774,9 +803,10 @@
     attend_back(0, 2)
     beat()
     attend_back(0, 1)
+    t1_arrive(1)
     beat()
     attend_back(1, 2)
-    beat()
+    t1_arrive(2)
     attend_back(1, 1)
 
     dq_core = remote(r["dq"].at[pl.ds(4 * e, 4)], r["dq"].at[pl.ds(4 * e, 4)], r["dq_cs"], r["dq_cr"], other)
@@ -790,18 +820,13 @@
     def tq_send(delta):
         return remote(r["tqs"].at[delta], cb.own.at[delta], (r["tq_s"], delta), (r["tq_r"], delta), dev(delta))
 
-    def dq_send(delta):
-        return remote(r["dqs"].at[delta], r["dqr"].at[delta], (r["dq_s"], delta), (r["dq_r"], delta), dev(delta))
+    def dq_send(delta, landing=None):
+        landing = chip if landing is None else landing
+        return remote(r["dqs"].at[delta], r["dqr"].at[landing], (r["dq_s"], delta), (r["dq_r"], delta), dev(delta))
 
     beat()
 
-    def t1_arrive(delta):
-        for half in (0, 1):
-            t1_send(delta, half).wait_recv()
-        ca.prime(8 + 2 * delta)
-        ca.prime(9 + 2 * delta)
-
-    t1_arrive(1)
+    t1_arrive(3)
     tq_core.wait_recv()
     for delta in (3, 2, 1, 0):
         c = chip_at(delta)
@@ -827,24 +852,28 @@
     def beat_to(count):
         beat(count - beats[0])
 
-    t1_arrive(2)
-    beat_to(13)
-    t1_arrive(3)
+    beat_to(12)
     cb.prime(0)
     beat_to(15)
     for delta in (1, 2, 3):
         tq_send(delta).wait_recv()
         cb.prime(delta)
     beat_to(18)
-    dn1 = mm_nt(r["dq"][r["inv"][b]], r["wo"][chip])
+    r["dqr"][chip] = r["dq"][r["inv"][b]]
     for delta in (1, 2, 3):
-        dq_send(delta).wait_recv()
-        dn1 += mm_nt(r["dqr"][delta], r["wo"][chip_at(delta)])
+        dq_send(delta, chip_at(delta)).wait_recv()
+    for i in range(4):
+        for t in range(3):
+            first = 768 * t + 192 * i
+            r["dnat"][:, first : first + 128] = r["dqr"][i, :, 128 * t : 128 * t + 128]
+            r["dnat"][:, first + 128 : first + 192] = r["dqr"][i, :, 384 + 64 * t : 448 + 64 * t]
+    dn1 = mm_nt(r["dnat"][...], r["wq"][...])
     hat, inv_std = norm_parts(r["xb"][b].astype(F32))
     r["lnp"][0:1] = jnp.sum(dn1 * hat, axis=0, keepdims=True)
     r["lnp"][1:2] = jnp.sum(dn1, axis=0, keepdims=True)
     r["lnp"][4:8] = jnp.zeros((4, 768), F32)
-    r["o_gin"][...] = (r["dx1"][...] + norm_back(dn1, hat, inv_std, g1)).astype(BF16)
+    r["s_gin"][...] = (r["dx1"][...] + norm_back(dn1, hat, inv_std, g1)).astype(BF16)
+    leave("gin", (slice(None),))
     ln_core = remote(r["lnp"], r["lnx"].at[0], (r["ln_s"], 0), (r["ln_r"], 0), other)
     ln_core.start()
     beat_to(19)
@@ -856,6 +885,7 @@
 
     for delta in (3, 2, 1):
         ln_send(delta).start()
+    beat_to(20)
     total = r["tps"][0].astype(F32)
     for delta in (1, 2, 3):
         tp_send(delta).wait_recv()
@@ -863,14 +893,19 @@
     for k in range(2):
         cp.own[k] = total[:, 384 * k : 384 * k + 384].astype(BF16)
         cp.prime(k)
-    beat_to(20)
     total = r["lns"][...]
     for delta in (1, 2, 3):
         ln_send(delta).wait_recv()
         total += r["lnx"][delta]
     cc.own[0] = total
     cc.prime(0)
-    beat_to(23 + SKEW * max(Z - 2, 0))
+    beat_to(22)
+    cc.tick(1)
+    beat_to(22 + SKEW)
+    cc.tick(1 + SKEW)
+    beat_to(22 + SKEW * max(Z - 2, 0))
+    for hop in range(2, max(Z - 2, 0) + 1):
+        cc.tick(1 + SKEW * hop)
 
     gx.finish(r["x"])
     gdy.finish(r["dy"])
@@ -891,42 +926,49 @@
     cb.finish()
     cp.finish()
     cc.finish()
+    for copy in leaving:
+        copy.wait()
 
 
 def widen_kernel(*refs):
     sources, results, held, wide = refs[:7], refs[7:17], refs[17:24], refs[24:32]
     sem_in, sem_out = refs[32:]
-    order = (4, 5, 2, 3, 6, 0, 1)
-    copies = {i: pltpu.make_async_copy(sources[i], held[i], sem_in.at[i]) for i in order}
-    for copy in copies.values():
-        copy.start()
+    every = slice(None)
+    pieces = [(4, (every, pl.ds(1024 * i, 1024))) for i in range(3)]
+    pieces += [(5, (pl.ds(128 * i, 128), every)) for i in range(3)]
+    pieces += [(2, (every,)), (3, (every,)), (6, (every,)), (0, (every,)), (1, (every,))]
+    copies = []
+    for n, (i, at) in enumerate(pieces):
+        copies.append(pltpu.make_async_copy(sources[i].at[at], held[i].at[at], sem_in.at[n]))
+        copies[-1].start()
     leaving = []
 
-    def leave(src, at):
-        copy = pltpu.make_async_copy(src, results[at], sem_out.at[at])
+    def leave(src, dst):
+        copy = pltpu.make_async_copy(src, dst, sem_out.at[len(leaving)])
         copy.start()
         leaving.append(copy)
 
-    for i in order:
-        copies[i].wait()
+    for (i, at), copy in zip(pieces, copies):
+        copy.wait()
         part = held[i]
         if i < 2:
-            leave(part, i)
+            leave(part, results[i])
         elif i == 2:
             for t in range(3):
                 parts = []
                 for c in range(4):
                     parts.append(part[c, :, 128 * t : 128 * t + 128])
                     parts.append(part[c, :, 384 + 64 * t : 448 + 64 * t])
-                wide[0][:, 768 * t : 768 * t + 768] = jnp.concatenate(parts, axis=1).astype(F32)
-            leave(wide[0], 2)
+                cols = (every, pl.ds(768 * t, 768))
+                wide[0][cols] = jnp.concatenate(parts, axis=1).astype(F32)
+                leave(wide[0].at[cols], results[2].at[cols])
         elif i < 6:
-            wide[i - 2][...] = part[...].astype(F32)
-            leave(wide[i - 2], i)
+            wide[i - 2][at] = part[at].astype(F32)
+            leave(wide[i - 2].at[at], results[i].at[at])
         else:
             for t in range(4):
                 wide[4 + t][...] = part[t, :]
-                leave(wide[4 + t], 6 + t)
+                leave(wide[4 + t], results[6 + t])
     for copy in leaving:
         copy.wait()
 
@@ -967,7 +1009,7 @@
         xb=V((8, 128, 768), BF16), gx_s=D((12,)), gx_r=D((12,)),
         dyb=V((8, 128, 768), BF16), gdy_s=D((12,)), gdy_r=D((12,)),
         dob=V((8, 128, 192), BF16), dos=V((4, 128, 192), BF16), do_s=D((8,)), do_r=D((8,)),
-        wq=V((768, 2304), BF16), wo=V((4, 768, 576), BF16), wp=V((768, 768), BF16),
+        wq=V((768, 2304), BF16), dnat=V((128, 2304), BF16), wp=V((768, 768), BF16),
         w1=V((768, 3072), BF16), w2=V((3072, 768), BF16),
         n1=V((8, 128, 768), BF16), n1s=V((4, 128, 768), BF16), qkv=V((8, 128, 1152), BF16),
         ob=V((2, 8, 128, 384), BF16), o_s=D((4,)), o_r=D((4,)),
@@ -993,12 +1035,13 @@
             scratch[name + "_" + part] = V((K, *shape), dtype)
         for part in ("su", "sd", "ru", "rd"):
             scratch[name + "_" + part] = D((K,))
+    scratch.update({"s" + name[1:]: V(*shape) for name, shape in results.items()}, out_sem=D((25,)))
     names = (*arguments, *results, *scratch)
     narrow = pl.pallas_call(
         functools.partial(layer_kernel, Z, names),
         out_shape=[jax.ShapeDtypeStruct(*shape) for shape in results.values()],
         in_specs=[spec for _, spec in arguments.values()],
-        out_specs=[vmem] * len(results),
+        out_specs=[anyspace] * len(results),
         scratch_shapes=list(scratch.values()),
         compiler_params=pltpu.CompilerParams(
             collective_id=0, has_side_effects=True, vmem_limit_bytes=60 * 2**20
@@ -1014,7 +1057,7 @@
         scratch_shapes=[V(*shape) for shape in results.values()]
         + [V(*shape) for shape in wide[2:6]]
         + [V((96,), F32)] * 4
-        + [D((len(narrow),)), D((len(wide),))],
+        + [D((11,)), D((16,))],
         compiler_params=pltpu.CompilerParams(vmem_limit_bytes=62 * 2**20),
     )(*narrow)
     return (y[None], gin[None], *grads)

time: 92 us -> 90 us (0.978)
  Pallas kernels: 91 us -> 89 us
    pallas_call x1, Pallas kernels: 87.8 us -> 85.8 us  [fast_shards(): pl.pallas_call(functools.partial(layer_kernel, Z, names), out_shape=[jax....]
where the time goes in v5:
time: 90 us; the launch traced here: 89.8 us
  Pallas kernels  89 us (99%)
    pallas_call x1, Pallas kernels, fast_shards(): pl.pallas_call(functools.partial(layer_kernel, Z, names), out_shape=[jax....  85.8 us
    pallas_call x1, Pallas kernels, fast_shards(): pl.pallas_call(widen_kernel, out_shape=[jax.ShapeDtypeStruct(*shape) for...  3.12 us

profile of v5, /device:TPU:0, one launch (start us, length us, event | category | flops | bytes accessed | tf_op | source)
XLA Modules:
  0.0 89.8 jit_solution(17326337223320957033)
XLA Ops:
  0.6 85.8 %shard_map.186 = (bf16[128,768]{1,0:T(8,128)(2,1)}, bf16[128,768]{1,0:T(8,128)(2,1)}, bf16[4,96,576]{2,1,0:T(8,128)(2,1)}, bf16[96,768]{1,0:T(8,128)(2,1)}, bf16...) custom-call(bf16[128,768]{1,0:T(8,128)(2,1)} %bitcast.4, s32[1,1024]{1,0:T(1,128)} %refs_1_.1, ...), custom_call_target="tpu_custom_call" | custom-call | tf_op jit(solution)/shard_map/pallas_call | solution.py:1040
  86.5 3.1 %shard_map.187 = (bf16[128,768]{1,0:T(8,128)(2,1)}, bf16[128,768]{1,0:T(8,128)(2,1)}, f32[96,2304]{1,0:T(8,128)}, f32[96,768]{1,0:T(8,128)}, f32[96,3072]{1,0:T(...) custom-call(bf16[128,768]{1,0:T(8,128)(2,1)} %get-tuple-element.27.refs_0_, ...), custom_call_target="tpu_custom_call" | custom-call | tf_op jit(solution)/shard_map/pallas_call | solution.py:1052

commit v6 on v5

--- a/solution.py
+++ b/solution.py
@@ -675,7 +675,7 @@
 
     for i in range(4):
         own_rows(i, 0)
-        if i == 3:
+        if i == 2:
             beat()
     r["s_y"][...] = r["y"][...].astype(BF16)
     leave("y", (slice(None),))

time: 90 us -> 88.7 us (0.986)
  Pallas kernels: 89 us -> 87.6 us
    pallas_call x1, Pallas kernels: 85.8 us -> 84.5 us  [fast_shards(): pl.pallas_call(functools.partial(layer_kernel, Z, names), out_shape=[jax....]
where the time goes in v6:
time: 88.7 us; the launch traced here: 88.5 us
  Pallas kernels  87.6 us (99%)
    pallas_call x1, Pallas kernels, fast_shards(): pl.pallas_call(functools.partial(layer_kernel, Z, names), out_shape=[jax....  84.5 us
    pallas_call x1, Pallas kernels, fast_shards(): pl.pallas_call(widen_kernel, out_shape=[jax.ShapeDtypeStruct(*shape) for...  3.12 us

profile of v6, /device:TPU:0, one launch (start us, length us, event | category | flops | bytes accessed | tf_op | source)
XLA Modules:
  0.0 88.5 jit_solution(8660591226207865915)
XLA Ops:
  0.6 84.5 %shard_map.186 = (bf16[128,768]{1,0:T(8,128)(2,1)}, bf16[128,768]{1,0:T(8,128)(2,1)}, bf16[4,96,576]{2,1,0:T(8,128)(2,1)}, bf16[96,768]{1,0:T(8,128)(2,1)}, bf16...) custom-call(bf16[128,768]{1,0:T(8,128)(2,1)} %bitcast.4, s32[1,1024]{1,0:T(1,128)} %refs_1_.1, ...), custom_call_target="tpu_custom_call" | custom-call | tf_op jit(solution)/shard_map/pallas_call | solution.py:1040
  85.2 3.1 %shard_map.187 = (bf16[128,768]{1,0:T(8,128)(2,1)}, bf16[128,768]{1,0:T(8,128)(2,1)}, f32[96,2304]{1,0:T(8,128)}, f32[96,768]{1,0:T(8,128)}, f32[96,3072]{1,0:T(...) custom-call(bf16[128,768]{1,0:T(8,128)(2,1)} %get-tuple-element.27.refs_0_, ...), custom_call_target="tpu_custom_call" | custom-call | tf_op jit(solution)/shard_map/pallas_call | solution.py:1052
